TPU v7x, 1024 devices: a whole 8x8x8 slice. The times are simulated.
1024 devices in a mesh: wave: 64 (over x, z), lev: 16 (over y, core).
Axes of the slice: x: 8, y: 8, z: 8, core: 2. Of those that a mesh axis runs over, the one named last changes fastest.
Arguments:
- spectrum: bfloat16 [1024, 1024, 96, 6], P('wave', None, 'lev'), may hold values from -0.3125 to 0.3125
- legendre: bfloat16 [1024, 1024, 128], P('wave'), may hold values from -0.1875 to 0.1875
- wave_numbers: int32 [1024], replicated, may hold values from 0 to 1023, as said below
- vertical: float32 [96, 96], replicated, may hold values from -0.625 to 0.625
Outputs:
- tracer: float32 [96, 256, 2048], P(None, 'wave', 'lev')
Inputs may be any that keep to these rules, and one draw needn't show every extreme that they name: wave_numbers is a permutation of 0 to 1023 in which slots 2 i and 2 i + 1 hold m and 1023 - m for some m, in either order.
All inputs are finite; a program needn't handle non-finite values.
Results may differ from a plain program's by a relative error of at most 0.0066.
Values may be sent and summed in bfloat16 or wider, within the bound.
A program may use at most 64 MiB of HBM per device.

v0:
```python
import math

import jax
import jax.numpy as jnp
from jax import lax
from jax.sharding import Mesh
from jax.sharding import PartitionSpec as P

NLON = 2048
LEV = ("lev_0", "lev_1")


courant_max = 0.45


def split_up(value, dim, length):
    before, after = (value.shape[:dim], value.shape[dim + 1 :])
    return jnp.moveaxis(value.reshape(*before, length, -1, *after), dim, 0)


def in_order(blocks, dim):
    blocks = jnp.moveaxis(blocks, 0, dim)
    shape = blocks.shape
    return blocks.reshape(*shape[:dim], shape[dim] * shape[dim + 1], *shape[dim + 2 :])


def exchange_in_order(blocks, axes, turns):
    shape = [lax.axis_size(a) for a in axes]
    blocks = blocks.reshape(*shape, *blocks.shape[1:])
    for k in turns:
        blocks = lax.all_to_all(blocks, axes[k], split_axis=k, concat_axis=k, tiled=True)
    return blocks.reshape(-1, *blocks.shape[len(axes) :])


def one_axis_at_a_time(value, axes, turns, split_dim, concat_dim):
    blocks = split_up(value, split_dim, lax.axis_size(axes))
    return in_order(exchange_in_order(blocks, axes, turns), concat_dim)


def padded(block, sides, width, periodic):
    for axis, dim in sides:
        count = lax.axis_size(axis)
        forward = [(i, i + 1) for i in range(count - 1)]
        if periodic:
            forward.append((count - 1, 0))
        backward = [(target, source) for source, target in forward]
        low = lax.ppermute(
            lax.slice_in_dim(block, block.shape[dim] - width, None, axis=dim), axis, forward
        )
        high = lax.ppermute(lax.slice_in_dim(block, 0, width, axis=dim), axis, backward)
        block = jnp.concatenate([low, block, high], axis=dim)
    return block


def twiddles(numbers):
    longitude = jnp.arange(NLON, dtype=jnp.int32)
    residue = numbers[:, None] * longitude[None, :] % NLON
    angles = residue.astype(jnp.float32) * (2.0 * math.pi / NLON)
    weight = jnp.where(numbers == 0, 1.0, 2.0).astype(jnp.float32)[:, None]
    return jnp.stack([weight * jnp.cos(angles), -weight * jnp.sin(angles)]).astype(jnp.bfloat16)


def parity_columns(coefficient, degree, lengths):
    counted = degree < lengths[:, None]
    even_mask = counted & (degree % 2 == 0)
    odd_mask = counted & (degree % 2 == 1)
    return jnp.concatenate(
        [
            jnp.where(even_mask[:, :, None], coefficient, 0),
            jnp.where(odd_mask[:, :, None], coefficient, 0),
        ],
        axis=2,
    )


def padded_sums(coefficient, basis, own_numbers):
    degree_count = coefficient.shape[1]
    degree = jnp.arange(degree_count, dtype=jnp.int32)[None, :]
    masked = parity_columns(coefficient, degree, degree_count - own_numbers)
    return jnp.einsum("skc,ski->sci", masked, basis, preferred_element_type=jnp.float32)


def upwind_core(extended, courant_x, courant_y):
    center = extended[:, 1:-1, 1:-1]
    western = extended[:, 1:-1, :-2]
    eastern = extended[:, 1:-1, 2:]
    northern = extended[:, :-2, 1:-1]
    southern = extended[:, 2:, 1:-1]
    return (
        center
        - jnp.maximum(courant_x, 0.0) * (center - western)
        - jnp.minimum(courant_x, 0.0) * (eastern - center)
        - jnp.maximum(courant_y, 0.0) * (center - northern)
        - jnp.minimum(courant_y, 0.0) * (southern - center)
    )


def body(spectrum, legendre, wave_numbers, vertical):
    slot_count, degree_count, level_count, part_count = spectrum.shape
    columns = level_count * part_count
    coefficient = spectrum.reshape(slot_count, degree_count, columns)
    first_slot = lax.axis_index("wave") * slot_count
    own_numbers = lax.dynamic_slice_in_dim(wave_numbers, first_slot, slot_count)
    partial_sums = padded_sums(coefficient, legendre, own_numbers)
    even_sums = partial_sums[:, :columns]
    odd_sums = partial_sums[:, columns:]
    northern = even_sums + odd_sums
    southern = jnp.flip(even_sums - odd_sums, axis=2)
    fourier = jnp.concatenate([northern, southern], axis=2).astype(jnp.bfloat16)
    received = lax.all_to_all(fourier, "wave", split_axis=2, concat_axis=0, tiled=True)
    lat_count = received.shape[2]
    received = received.reshape(received.shape[0], level_count, 3, 2, lat_count)
    twiddle = twiddles(wave_numbers)
    grid_values = jnp.einsum(
        "smfrl,rsj->lmfj", received, twiddle, preferred_element_type=jnp.float32
    ).astype(jnp.bfloat16)
    column_values = one_axis_at_a_time(grid_values, LEV, (1, 0), 3, 1)
    fields = jnp.einsum(
        "vm,lmfj->fvlj",
        vertical,
        column_values.astype(jnp.float32),
        precision=lax.Precision.HIGHEST,
    )
    courant_x = courant_max * jnp.tanh(fields[0])
    courant_y = courant_max * jnp.tanh(fields[1])
    tracer = fields[2]
    stacked = jnp.stack([tracer, courant_x, courant_y])
    extended = padded(stacked, (("wave", 2),), 2, False)
    extended = padded(extended, ((LEV, 3),), 2, True)
    first_step = upwind_core(extended[0], extended[1][:, 1:-1, 1:-1], extended[2][:, 1:-1, 1:-1])
    band_index = lax.axis_index("wave")
    band_count = lax.axis_size("wave")
    row_count = first_step.shape[1]
    row_index = jnp.arange(row_count, dtype=jnp.int32)
    inside = ((row_index > 0) | (band_index > 0)) & (
        (row_index < row_count - 1) | (band_index < band_count - 1)
    )
    first_step = jnp.where(inside[None, :, None], first_step, 0.0)
    tracer = upwind_core(first_step, extended[1][:, 2:-2, 2:-2], extended[2][:, 2:-2, 2:-2])
    return tracer


def solution(mesh):
    split = Mesh(mesh.devices.reshape(mesh.shape["wave"], 8, 2), ("wave", "lev_0", "lev_1"))
    placed = (P("wave", None, LEV, None), P("wave", None, None), P(), P())
    return jax.shard_map(
        body, mesh=split, in_specs=placed, out_specs=P(None, "wave", LEV), check_vma=False
    )
```

profile of v0, /device:TPU:8, one launch (start us, length us, event | category | flops | bytes accessed | tf_op | source)
XLA Modules:
  0.0 139.0 jit_solution(14506322428106925342)
XLA Ops:
  0.0 0.0 copy-start
  0.0 0.8 dynamic-slice_subtract_fusion
  0.8 0.1 fusion.36
  0.9 2.8 %broadcast_select_fusion.1 = (bf16[16,1024,36]{1,2,0:T(8,128)(2,1)S(1)}, bf16[16,1024,36]{1,2,0:T(8,128)(2,1)S(1)}) fusion(pred[16,1024]{1,0:T(8,128)(4,1)S(1)} %get-tuple-element.21, bf16[16,1024,36]{1,0,2:T(8,128)(2,1)} %bitcast.62, pred[16,1024]{1,0:T(8,128)(4,1)S(1)} %get-tuple-element.22), kind=kLoop, calls=%fused_computation.22 | loop fusion | flops 1179648 | bytes 3571712 | tf_op jit(solution)/shard_map/jit(_where)/select_n | solution.py:69
  3.6 3.1 %fusion.8 = f32[16,72,128]{2,1,0:T(8,128)S(1)} fusion(bf16[16,1024,128]{2,1,0:T(8,128)(2,1)} %param.5, bf16[16,1024,36]{1,2,0:T(8,128)(2,1)S(1)} %get-tuple-element.11, bf16[16,1024,36]{1,2,0:T(8,128)(2,1)S(1)} %get-tuple-element.10), kind=kOutput, calls=%fused_computation.14 | convolution fusion | flops 306708480 | bytes 7143424 | tf_op jit(solution)/shard_map/skc,ski->sci/dot_general | solution.py:80
  6.8 0.0 copy-start.1
  6.9 0.1 rev.4
  7.1 1.0 copy.39
  8.1 3.2 %reshape.258 = bf16[64,2,1152]{2,1,0:T(2,128)(2,1)} reshape(bf16[256,16,36]{2,1,0:T(8,128)(2,1)S(1)} %bitcast.57) | data formatting | bytes 589824
  11.3 22.7 %all-to-all-start = ((bf16[64,2,1152]{2,1,0:T(2,128)(2,1)}), bf16[64,2,1152]{2,1,0:T(2,128)(2,1)S(1)}, u32[]{:S(2)}, u32[]{:S(2)}) async-start(bf16[64,2,1152]{2,1,0:T(2,128)(2,1)} %reshape.258), calls=%async_computation | async-start | bytes 589824 | tf_op jit(solution)/shard_map/all_to_all | solution.py:110
  34.0 0.0 copy-done.1
  34.0 37.3 %multiply_convert_fusion.1 = (bf16[1,1024,2048]{2,1,0:T(8,128)(2,1)}, bf16[1,1024,2048]{2,1,0:T(8,128)(2,1)}) fusion(s32[1024]{0:T(1024)S(1)} %copy-done.1, f32[1024]{0:T(1024)S(1)} %get-tuple-element.19, f32[1024]{0:T(1024)S(1)} %get-tuple-element.20), kind=kLoop, calls=%fused_computation.8 | loop fusion | flops 37748736 | bytes 8400896 | tf_op jit(solution)/shard_map/convert.2
  71.3 0.0 all-to-all-done
  71.3 3.0 %reshape.259 = bf16[256,16,36]{2,1,0:T(8,128)(2,1)S(1)} reshape(bf16[64,2,1152]{2,1,0:T(2,128)(2,1)S(1)} %all-to-all-done) | data formatting | bytes 589824
  74.3 5.4 %copy.40 = bf16[64,16,36,4]{1,0,3,2:T(8,128)(2,1)S(1)} copy(bf16[64,16,36,4]{2,1,3,0:T(8,128)(2,1)S(1)} %bitcast.58) | data formatting | bytes 589824 | tf_op jit(solution)/shard_map/all_to_all | solution.py:110
  79.7 2.6 %reshape.249 = bf16[1024,6,3,2,4]{0,4,3,2,1:T(4,128)(2,1)S(1)} reshape(bf16[64,16,36,4]{1,0,3,2:T(8,128)(2,1)S(1)} %copy.40) | data formatting | bytes 589824 | tf_op jit(solution)/shard_map/reshape | solution.py:112
  82.3 4.4 %fusion.13 = bf16[4,6,3,2048]{3,1,0,2:T(8,128)(2,1)S(1)} fusion(bf16[1,1024,2048]{2,1,0:T(8,128)(2,1)} %get-tuple-element.18, bf16[1,1024,2048]{2,1,0:T(8,128)(2,1)} %get-tuple-element.17, bf16[1024,6,3,2,4]{0,4,3,2,1:T(4,128)(2,1)S(1)} %reshape.249), kind=kOutput, calls=%fused_computation.20 | convolution fusion | flops 620904448 | bytes 8978432 | tf_op jit(solution)/shard_map/smfrl,rsj->lmfj/dot_general | solution.py:114
  86.7 0.4 reshape.257
  87.1 4.0 %all_to_all.25 = bf16[8,2,4,6,3,128]{5,0,2,4,3,1:T(8,128)(2,1)S(1)} all-to-all(bf16[8,2,4,6,3,128]{5,0,2,4,3,1:T(8,128)(2,1)S(1)} %copy.43), channel_id=1, replica_groups=mesh['wave'=64,'lev_0'=8,'lev_1'=2] {'lev_1'}, dimensions={1} | all-to-all | bytes 589824 | tf_op jit(solution)/shard_map/all_to_all | solution.py:31
  91.1 0.3 copy.44
  91.4 20.2 %all_to_all.26 = bf16[8,2,4,6,3,128]{5,1,2,4,3,0:T(2,128)(2,1)S(1)} all-to-all(bf16[8,2,4,6,3,128]{5,1,2,4,3,0:T(2,128)(2,1)S(1)} %copy.44), channel_id=1, replica_groups=mesh['wave'=64,'lev_0'=8,'lev_1'=2] {'lev_0'}, dimensions={0} | all-to-all | bytes 589824 | tf_op jit(solution)/shard_map/all_to_all | solution.py:31
  111.6 0.2 copy.45
  111.8 0.2 copy.46
  112.0 0.0 copy-done
  112.0 0.4 convolution_bitcast_fusion
  112.4 0.1 fusion.48
  112.6 3.4 %collective-permute-start = (f32[3,96,2,128]{3,1,0,2:T(8,128)S(1)}, f32[3,96,2,128]{3,1,0,2:T(8,128)S(1)}, u32[]{:S(2)}, u32[]{:S(2)}) collective-permute-start(f32[3,96,2,128]{3,1,0,2:T(8,128)S(1)} %get-tuple-element.12), channel_id=1, source_target_pairs={{0,16},{16,32},{32,48},{48,64},{64,80},{80,96},{96,112},{112,128},... | collective-permute-start | bytes 884744 | tf_op jit(solution)/shard_map/ppermute | solution.py:47
  115.9 6.0 %collective-permute-start.1 = (f32[3,96,2,128]{3,1,0,2:T(8,128)S(1)}, f32[3,96,2,128]{3,1,0,2:T(8,128)}, u32[]{:S(2)}, u32[]{:S(2)}) collective-permute-start(f32[3,96,2,128]{3,1,0,2:T(8,128)S(1)} %get-tuple-element.13), channel_id=1, source_target_pairs={{16,0},{32,16},{48,32},{64,48},{80,64},{96,80},{112,96},{128,112},... | collective-permute-start | bytes 884744 | tf_op jit(solution)/shard_map/ppermute | solution.py:50
  122.0 3.9 %collective-permute-done = f32[3,96,2,128]{3,1,0,2:T(8,128)S(1)} collective-permute-done((f32[3,96,2,128]{3,1,0,2:T(8,128)S(1)}, f32[3,96,2,128]{3,1,0,2:T(8,128)S(1)}, u32[]{:S(2)}, u32[]{:S(2)}) %collective-permute-start) | collective-permute-done | bytes 294944 | tf_op jit(solution)/shard_map/ppermute | solution.py:47
  125.9 1.2 collective-permute-done.1
  127.0 1.0 pad_maximum_fusion.1
  128.1 0.4 fusion.46
  128.5 0.4 copy.48
  128.9 0.4 copy.49
  129.3 0.0 collective-permute-start.3
  129.3 0.5 collective-permute-start.2
  129.8 3.9 %collective-permute-done.2 = f32[3,96,8,2]{1,2,3,0:T(8,128)S(1)} collective-permute-done((f32[3,96,8,2]{1,2,3,0:T(8,128)S(1)}, f32[3,96,8,2]{1,2,3,0:T(8,128)S(1)}, u32[]{:S(2)}, u32[]{:S(2)}) %collective-permute-start.2) | collective-permute-done | bytes 18464 | tf_op jit(solution)/shard_map/ppermute | solution.py:47
  133.8 0.4 copy.50
  134.2 0.0 collective-permute-done.3
  134.2 0.4 copy.51
  134.6 1.9 %pad_maximum_fusion = f32[3,96,8,132]{3,1,0,2:T(8,128)S(1)} fusion(f32[3,96,8,2]{3,1,0,2:T(8,128)S(1)} %copy.51, f32[3,96,2,128]{3,1,0,2:T(8,128)} %collective-permute-done.1, f32[1,96,4,128]{3,1,0,2:T(8,128)S(1)} %get-tuple-element.15, f32[1,96,4,128]{3,1,0,2:T(8,128)S(1)} %get-tuple-element.16, f32[1,96,4,128]{3,1,0,2:T(8,128)S(1)} %get-tuple-element.14, ...), kind=kLoop, calls=%fused_computation.18 | loop fusion | flops 1824768 | bytes 2433024 | tf_op jit(solution)/shard_map/concatenate | solution.py:51
  136.6 0.2 slice_bitcast_fusion.1
  136.8 1.0 fusion.16
  137.8 0.4 fusion.26
  138.2 0.8 copy.54
  (10 shorter events, 0.3 us)
Async XLA Ops:
  0.0 112.0 %copy-start = (f32[96,96]{1,0:T(8,128)S(1)}, f32[96,96]{1,0:T(8,128)}, u32[]{:S(2)}) copy-start(f32[96,96]{1,0:T(8,128)} %param.7) | copy-start | bytes 110596
  6.8 27.2 %copy-start.1 = (s32[1024]{0:T(1024)S(1)}, s32[1024]{0:T(1024)}, u32[]{:S(2)}) copy-start(s32[1024]{0:T(1024)} %param.6) | copy-start | bytes 12292
  11.3 60.0 %all-to-all-start = ((bf16[64,2,1152]{2,1,0:T(2,128)(2,1)}), bf16[64,2,1152]{2,1,0:T(2,128)(2,1)S(1)}, u32[]{:S(2)}, u32[]{:S(2)}) async-start(bf16[64,2,1152]{2,1,0:T(2,128)(2,1)} %reshape.258), calls=%async_computation | async-start | bytes 589824 | tf_op jit(solution)/shard_map/all_to_all | solution.py:110
  112.6 13.3 %collective-permute-start = (f32[3,96,2,128]{3,1,0,2:T(8,128)S(1)}, f32[3,96,2,128]{3,1,0,2:T(8,128)S(1)}, u32[]{:S(2)}, u32[]{:S(2)}) collective-permute-start(f32[3,96,2,128]{3,1,0,2:T(8,128)S(1)} %get-tuple-element.12), channel_id=1, source_target_pairs={{0,16},{16,32},{32,48},{48,64},{64,80},{80,96},{96,112},{112,128},... | collective-permute-start | bytes 884744 | tf_op jit(solution)/shard_map/ppermute | solution.py:47
  115.9 11.1 %collective-permute-start.1 = (f32[3,96,2,128]{3,1,0,2:T(8,128)S(1)}, f32[3,96,2,128]{3,1,0,2:T(8,128)}, u32[]{:S(2)}, u32[]{:S(2)}) collective-permute-start(f32[3,96,2,128]{3,1,0,2:T(8,128)S(1)} %get-tuple-element.13), channel_id=1, source_target_pairs={{16,0},{32,16},{48,32},{64,48},{80,64},{96,80},{112,96},{128,112},... | collective-permute-start | bytes 884744 | tf_op jit(solution)/shard_map/ppermute | solution.py:50
  129.3 4.9 %collective-permute-start.3 = (f32[3,96,8,2]{1,2,3,0:T(8,128)S(1)}, f32[3,96,8,2]{1,2,3,0:T(8,128)S(1)}, u32[]{:S(2)}, u32[]{:S(2)}) collective-permute-start(f32[3,96,8,2]{1,2,3,0:T(8,128)S(1)} %copy.49), channel_id=1, source_target_pairs={{1,0},{2,1},{3,2},{4,3},{5,4},{6,5},{7,6},{8,7},{9,8},{10,9},{11,1... | collective-permute-start | bytes 55304 | tf_op jit(solution)/shard_map/ppermute | solution.py:50
  129.3 4.5 %collective-permute-start.2 = (f32[3,96,8,2]{1,2,3,0:T(8,128)S(1)}, f32[3,96,8,2]{1,2,3,0:T(8,128)S(1)}, u32[]{:S(2)}, u32[]{:S(2)}) collective-permute-start(f32[3,96,8,2]{1,2,3,0:T(8,128)S(1)} %copy.48), channel_id=1, source_target_pairs={{0,1},{1,2},{2,3},{3,4},{4,5},{5,6},{6,7},{7,8},{8,9},{9,10},{10,1... | collective-permute-start | bytes 55304 | tf_op jit(solution)/shard_map/ppermute | solution.py:47
where the time goes:
time: 139 us
  other arithmetic  45.5 us (33%)
  starting transfers between devices  32.6 us (23%)
  blocking collectives  24.2 us (17%)
  local copies, waits for them, and re-layouts  19.5 us (14%)
  waiting for transfers between devices  9.03 us (6%)
  matrix products  7.85 us (6%)
    another operation x2, other arithmetic  37.3 us
    all_to_all x2, blocking collectives, exchange_in_order(): lax.all_to_all(blocks, axes[k], split_axis=k, concat_axis=k, tiled=True)  24.2 us
    all_to_all x1, starting transfers between devices, body(): lax.all_to_all(fourier, 'wave', split_axis=2, concat_axis=0, tiled=True)  22.7 us
    ppermute x2, waiting for transfers between devices, padded(): lax.ppermute(lax.slice_in_dim(block, block.shape[dim] - width, None, axis...  7.85 us
    unnamed x6, local copies, waits for them, and re-layouts  6.18 us
    ppermute x2, starting transfers between devices, padded(): lax.ppermute(lax.slice_in_dim(block, 0, width, axis=dim), axis, backward)  6 us
    all_to_all x1, local copies, waits for them, and re-layouts, body(): lax.all_to_all(fourier, 'wave', split_axis=2, concat_axis=0, tiled=True)  5.4 us
    dot_general x1, matrix products, body(): jnp.einsum('smfrl,rsj->lmfj', received, twiddle, preferred_element_type=j...  4.35 us
  transfers between devices with their start and end apart: 5, of which 3 were waited for; matrix products, arithmetic and copies ran while one was open for 27% of the time, Pallas kernels for 0%

commit v1 on v0

v1 whole, which is shorter than its diff:
```python
import jax
import jax.numpy as jnp
import numpy as np
from jax import lax
from jax.experimental import pallas as pl
from jax.experimental.pallas import tpu as pltpu
from jax.sharding import PartitionSpec as P

BF = jnp.bfloat16
F32 = jnp.float32
MESH = pl.DeviceIdType.MESH
COURANT = 0.45

NM = 1024
NLON = 2048
LEVS = 96
WAVES = 64
LEVDEV = 16
SLOTS = 16
COLS = 36
MODES = 6
RADIX = 8
SPAN = NLON // RADIX

GROUPS = (
    ((0, 1), (1, 1), (0, 2), (1, 2)),
    ((0, 0), (1, 0), (2, 0), (2, 1)),
    ((2, 2), (2, 3), (1, 3), (0, 3)),
)
PLACE = {pair: (g, i) for g, group in enumerate(GROUPS) for i, pair in enumerate(group)}
EDGE_TILE = 6
OFFSETS = (-2, -1, 0, 127, 128, 129)


def fourier_table():
    numbers = np.arange(NM).reshape(NM // RADIX, RADIX).T
    residue = numbers[:, :, None] * np.arange(SPAN)[None, None, :] % NLON
    angle = residue * (2.0 * np.pi / NLON)
    weight = np.where(numbers == 0, 1.0, 2.0)[:, :, None]
    real, imaginary = weight * np.cos(angle), weight * np.sin(angle)
    imaginary = np.where(residue == 0, 0.0, imaginary)
    top = np.concatenate([real, imaginary], axis=2)
    bottom = np.concatenate([-imaginary, real], axis=2)
    return np.concatenate([top, bottom], axis=1).astype(BF)


def row_table():
    table = np.zeros((144, 256), np.float32)
    for (field, lat), (group, place) in PLACE.items():
        for mode in range(MODES):
            for part in range(2):
                pair = mode * 3 + field
                if pair < 16:
                    column = part * 64 + lat * 16 + pair
                else:
                    column = 128 + lat * 4 + (pair - 16) * 2 + part
                table[part * 72 + group * 24 + mode * 4 + place, column] = 1.0
    return table.astype(BF)


def edge_table():
    table = np.zeros((NLON, 128), np.float32)
    for block in range(LEVDEV):
        for k, offset in enumerate(OFFSETS):
            table[(block * 128 + offset) % NLON, block * 8 + k] = 1.0
    return table.astype(BF)


def spread_table():
    table = np.zeros((LEVS, 128), np.float32)
    for mode in range(LEVS):
        table[mode, mode // MODES * 8 + mode % MODES] = 1.0
    return table.astype(BF)


def dot(a, b):
    return jnp.dot(a, b, preferred_element_type=F32)


def pick(values, index):
    result = values[-1]
    for i in range(len(values) - 2, -1, -1):
        result = jnp.where(index == i, values[i], result)
    return result


def legendre_stage(numbers, spec, leg, copies, main, rest, wide, turned, tall, gather):
    for c in range(COLS + 4):
        values = spec[c if c < COLS else c - 4].astype(F32)
        for k in range(8):
            wide[k, c * SLOTS : (c + 1) * SLOTS, :] = values[:, k * 128 : (k + 1) * 128]
    degree = lax.broadcasted_iota(jnp.int32, (40, NM), 1)
    odd = degree % 2 == 1
    lane = lax.broadcasted_iota(jnp.int32, (32, 128), 1)
    turn = lane // 16 % 4
    small = lane // 4 % 4
    for s in range(SLOTS):
        if s % 4 == 0:
            copies[s // 4].wait()
        rows = jnp.concatenate(
            [
                jnp.concatenate(
                    [
                        wide[k, pl.ds(s, 16, stride=32), :],
                        wide[k, pl.ds(16 + s, 16, stride=32), :],
                        wide[k, pl.ds(512 + s, 8, stride=16), :],
                    ],
                    axis=0,
                )
                for k in range(8)
            ],
            axis=1,
        )
        rows = jnp.where(degree < NM - numbers(s), rows, 0.0)
        both = jnp.concatenate([rows, jnp.where(odd, -rows, rows)], axis=0).astype(BF)
        sums = dot(both, leg[s])
        for half in range(2):
            own = sums[half * 40 : (half + 1) * 40]
            block = jnp.concatenate([own[0:16]] * 4 + [own[16:32]] * 4, axis=0)
            turned[half, s % 2] = block.T
            lines = [turned[half, s % 2, pl.ds(r, 32, stride=4), :] for r in range(4)]
            if half == 1:
                lines = lines[::-1]
            gather[pl.ds(half * 512 + s, 32, stride=SLOTS), :] = pick(lines, turn)
            tall[half, s * 16 : (s + 1) * 16, :] = jnp.concatenate([own[32:40]] * 2, axis=0)
    for half in range(2):
        for h in range(2):
            turned[half, h] = tall[half, h * 128 : (h + 1) * 128, :].T
            lines = [turned[half, h, pl.ds(r, 32, stride=4), :] for r in range(4)]
            if half == 1:
                lines = lines[::-1]
            rest[half * 32 : (half + 1) * 32, h, :] = pick(lines, small)
    for b in range(WAVES):
        main[b] = gather[b * SLOTS : (b + 1) * SLOTS, :].astype(BF)


def choose_rows(numbers, choice):
    line = lax.broadcasted_iota(jnp.int32, (32, NM), 0)

    def step(i, carry):
        wanted = i // 4 + RADIX * (i % 4 * 32 + line)
        hit = jnp.where(numbers == wanted, 1.0, 0.0).astype(BF)
        choice[pl.ds(pl.multiple_of(i * 32, 32), 32), :] = hit
        return carry

    lax.fori_loop(0, 32, step, 0)


def fourier_stage(main, rest, choice, order, table, edges, message, small, joined, part, grid, edge):
    joined[:, 0:128] = main[...].reshape(NM, 128)
    for h in range(2):
        values = rest[:, h, :]
        for g in range(8):
            rolled = values if g == 0 else pltpu.roll(values, 128 - 16 * g, 1)
            small[pl.ds(h * 8 + g, WAVES, stride=SLOTS), :] = rolled
    joined[:, 128:256] = small[...].astype(BF)
    ordered = dot(choice[...], joined[...]).astype(BF)
    lines = lax.dot_general(
        order[...], ordered, (((1,), (1,)), ((), ())), preferred_element_type=F32
    )
    for k in range(RADIX):
        own = lines[:, k * 128 : (k + 1) * 128]
        pair = jnp.concatenate([own[0:72].astype(BF), own[72:144].astype(BF)], axis=1)
        part[k] = dot(pair, table[k])
    root = 0.5**0.5

    def combine(i, carry):
        row = pl.ds(pl.multiple_of(i * 8, 8), 8)
        tile = i + jnp.where(i >= EDGE_TILE, 1, 0)
        for h in range(2):
            re = [part[k, row, h * 128 : (h + 1) * 128] for k in range(RADIX)]
            im = [
                None if k % 4 == 0 else part[k, row, SPAN + h * 128 : SPAN + (h + 1) * 128]
                for k in range(RADIX)
            ]
            plus, minus = re[0] + re[4], re[0] - re[4]
            level, cross = re[2] + re[6], im[6] - im[2]
            even = [plus + level, minus + cross, plus - level, minus - cross]
            a, b = re[1] - re[5], re[7] - re[3]
            c, d = im[5] - im[1], im[7] - im[3]
            odd = [
                re[1] + re[3] + re[5] + re[7],
                root * (a + b + c + d),
                im[3] - im[1] + im[7] - im[5],
                root * (c + d - a - b),
            ]
            for u in range(RADIX):
                value = even[u % 4] + odd[u] if u < 4 else even[u % 4] - odd[u - 4]
                message[2 * u + h, tile] = value.astype(BF)
                grid[row, u * SPAN + h * 128 : u * SPAN + (h + 1) * 128] = value
        return carry

    lax.fori_loop(0, 9, combine, 0)
    edge[0:72] = dot(grid[...].astype(BF), edges[...])
    edge[72:80] = jnp.zeros((8, 128), F32)
    lane = lax.broadcasted_iota(jnp.int32, (8, 128), 1) // 8

    def pack(block, carry):
        total = jnp.zeros((8, 128), F32)
        for field in range(3):
            for lat in range(4):
                group, place = PLACE[(field, lat)]
                q = field * 4 + lat
                values = edge[pl.ds(group * 24 + place, 8, stride=4), :]
                rolled = pltpu.roll(values, (128 + 8 * q - 8 * block) % 128, 1)
                total = jnp.where(lane == q, rolled, total)
        message[block, EDGE_TILE] = total.astype(BF)
        return carry

    lax.fori_loop(0, LEVDEV, pack, 0)


def vertical_stage(band, own, north, south, vertical, spread, out, wide, fields, edges):
    sources = ((own, 0), (own, 3), (own, 7), (north, 1), (south, 0))
    for i, (ref, tile) in enumerate(sources):
        for d in range(LEVDEV):
            values = ref[d, tile : tile + 3].astype(F32)
            wide[i, d * 24 : (d + 1) * 24, :] = values.reshape(24, 128)
    top = vertical[...].astype(BF)
    low = (vertical[...] - top.astype(F32)).astype(BF)
    both = jnp.concatenate([top, low], axis=0)
    for i in range(5):
        for q in range(0, 4, 2):
            modes = jnp.concatenate(
                [wide[i, pl.ds(q, LEVS, stride=4), :], wide[i, pl.ds(q + 1, LEVS, stride=4), :]],
                axis=1,
            ).astype(BF)
            twice = dot(both, modes)
            value = twice[:LEVS] + twice[LEVS:]
            fields[i, q] = value[:, :128]
            fields[i, q + 1] = value[:, 128:]
    both = dot(both, spread[...]).astype(BF)
    for i, (ref, tile) in enumerate(((own, EDGE_TILE), (north, 0), (south, 3))):
        values = ref[:, tile].reshape(128, 128)
        twice = dot(both, values)
        edges[i] = twice[:LEVS] + twice[LEVS:]

    lane = lax.broadcasted_iota(jnp.int32, (8, 128), 1)
    first, last = band == 0, band == WAVES - 1

    def where_is(field, lat):
        if lat < 0:
            group, place = PLACE[(field, lat + 4)]
            return 3, place
        if lat > 3:
            group, place = PLACE[(field, lat - 4)]
            return 4, place
        return PLACE[(field, lat)]

    def shift(value, amount):
        amount = amount % 128
        return value if amount == 0 else pltpu.roll(value, amount, 1)

    def upwind(center, west, east, north, south, cx, cy):
        return (
            center
            - jnp.maximum(cx, 0.0) * (center - west)
            - jnp.minimum(cx, 0.0) * (east - center)
            - jnp.maximum(cy, 0.0) * (center - north)
            - jnp.minimum(cy, 0.0) * (south - center)
        )

    def line(step, carry):
        level = pl.ds(pl.multiple_of(step * 8, 8), 8)

        def field(f, lat):
            i, q = where_is(f, lat)
            return fields[i, q, level, :]

        def courant(value):
            return COURANT * jnp.tanh(value)

        zero = jnp.zeros((8, 128), F32)
        tracer = {lat: field(2, lat) for lat in range(-2, 6)}
        for lat in (-2, -1):
            tracer[lat] = jnp.where(first, zero, tracer[lat])
        for lat in (4, 5):
            tracer[lat] = jnp.where(last, zero, tracer[lat])
        cx = {lat: courant(field(0, lat)) for lat in range(-1, 5)}
        cy = {lat: courant(field(1, lat)) for lat in range(-1, 5)}
        mine, upper, lower = edges[0, level, :], edges[1, level, :], edges[2, level, :]

        def side(f):
            return jnp.where(
                lane < 16,
                shift(upper, -(f * 32 + 16)),
                jnp.where(lane < 48, shift(mine, 16 - f * 32), shift(lower, 48 - f * 32)),
            )

        edge = side(2)
        edge = jnp.where(((lane < 16) & first) | ((lane >= 48) & last), zero, edge)
        edge_x, edge_y = courant(side(0)), courant(side(1))

        def beside(value, rim, lat):
            west = shift(value, 1)
            west = jnp.where(lane == 0, shift(rim, -((lat + 2) * 8 + 1)), west)
            east = shift(value, -1)
            east = jnp.where(lane == 127, shift(rim, 127 - ((lat + 2) * 8 + 4)), east)
            return west, east

        once = {}
        for lat in range(-1, 5):
            west, east = beside(tracer[lat], edge, lat)
            once[lat] = upwind(
                tracer[lat], west, east, tracer[lat - 1], tracer[lat + 1], cx[lat], cy[lat]
            )
        once[-1] = jnp.where(first, zero, once[-1])
        once[4] = jnp.where(last, zero, once[4])
        rim = upwind(
            edge, shift(edge, 1), shift(edge, -1), shift(edge, 8), shift(edge, -8), edge_x, edge_y
        )
        for lat in range(4):
            west, east = beside(once[lat], rim, lat)
            out[level, lat, :] = upwind(
                once[lat], west, east, once[lat - 1], once[lat + 1], cx[lat], cy[lat]
            )
        return carry

    lax.fori_loop(0, LEVS // 8, line, 0)


def kernel_a(numbers, spec, leg, main, rest, leg_here, sem, wide, turned, tall, gather):
    copies = []
    for i in range(4):
        copy = pltpu.make_async_copy(
            leg.at[4 * i : 4 * i + 4], leg_here.at[4 * i : 4 * i + 4], sem.at[i]
        )
        copy.start()
        copies.append(copy)
    first = lax.axis_index("wave") * SLOTS
    legendre_stage(
        lambda s: numbers[first + s], spec, leg_here, copies, main, rest, wide, turned, tall, gather
    )


def send_rows(w):
    return jnp.where(w < WAVES // 2, w, 95 - w)


def kernel_t1(main, rest, main_out, rest_out, send, recv, here):
    w = lax.axis_index("wave")
    barrier = pltpu.get_barrier_semaphore()

    def greet(i, carry):
        pl.semaphore_signal(
            barrier, inc=1, device_id={"wave": lax.rem(w + i, WAVES)}, device_id_type=MESH
        )
        return carry

    lax.fori_loop(1, WAVES, greet, 0)
    pl.semaphore_wait(barrier, WAVES - 1)

    def go(i, carry):
        target = lax.rem(w + i, WAVES)
        row = send_rows(target)
        for j, (src, dst) in enumerate(((main, main_out), (rest, rest_out))):
            pltpu.make_async_remote_copy(
                src_ref=src.at[row],
                dst_ref=dst.at[w],
                send_sem=send.at[j],
                recv_sem=recv.at[j],
                device_id={"wave": target},
                device_id_type=MESH,
            ).start()
        return carry

    lax.fori_loop(1, WAVES, go, 0)
    row = send_rows(w)
    local = [
        pltpu.make_async_copy(src.at[row], dst.at[w], here.at[j])
        for j, (src, dst) in enumerate(((main, main_out), (rest, rest_out)))
    ]
    for copy in local:
        copy.start()
    for copy in local:
        copy.wait()
    many = pl.ds(0, WAVES - 1)
    for j, (src, dst) in enumerate(((main, main_out), (rest, rest_out))):
        whole = pltpu.make_async_remote_copy(
            src_ref=src.at[many],
            dst_ref=dst.at[many],
            send_sem=send.at[j],
            recv_sem=recv.at[j],
            device_id={"wave": lax.rem(w + 1, WAVES)},
            device_id_type=MESH,
        )
        whole.wait_send()
        whole.wait_recv()


def kernel_b(main, rest, numbers, order, table, edges, message, choice, small, joined, part, grid, edge):
    choose_rows(numbers[...], choice)
    fourier_stage(
        main, rest, choice, order, table, edges, message, small, joined, part, grid, edge
    )


def kernel_t2(message, own, north, south, send, recv, here, halo_send, halo_recv):
    w, v = lax.axis_index("wave"), lax.axis_index("lev")
    barrier = pltpu.get_barrier_semaphore()

    def greet(i, carry):
        pl.semaphore_signal(
            barrier, inc=1, device_id={"lev": lax.rem(v + i, LEVDEV)}, device_id_type=MESH
        )
        return carry

    lax.fori_loop(1, LEVDEV, greet, 0)
    upper, lower = lax.rem(w + WAVES - 1, WAVES), lax.rem(w + 1, WAVES)
    for other in (upper, lower):
        pl.semaphore_signal(barrier, inc=1, device_id={"wave": other}, device_id_type=MESH)
    pl.semaphore_wait(barrier, LEVDEV + 1)

    def go(i, carry):
        target = lax.rem(v + i, LEVDEV)
        pltpu.make_async_remote_copy(
            src_ref=message.at[target],
            dst_ref=own.at[v],
            send_sem=send,
            recv_sem=recv,
            device_id={"lev": target},
            device_id_type=MESH,
        ).start()
        return carry

    lax.fori_loop(1, LEVDEV, go, 0)
    local = pltpu.make_async_copy(message.at[v], own.at[v], here)
    local.start()
    local.wait()
    many = pl.ds(0, LEVDEV - 1)
    whole = pltpu.make_async_remote_copy(
        src_ref=message.at[many],
        dst_ref=own.at[many],
        send_sem=send,
        recv_sem=recv,
        device_id={"lev": lax.rem(v + 1, LEVDEV)},
        device_id_type=MESH,
    )
    whole.wait_send()
    whole.wait_recv()
    down = pltpu.make_async_remote_copy(
        src_ref=own.at[:, 6:10],
        dst_ref=north,
        send_sem=halo_send.at[0],
        recv_sem=halo_recv.at[0],
        device_id={"wave": lower},
        device_id_type=MESH,
    )
    up = pltpu.make_async_remote_copy(
        src_ref=own.at[:, 3:7],
        dst_ref=south,
        send_sem=halo_send.at[1],
        recv_sem=halo_recv.at[1],
        device_id={"wave": upper},
        device_id_type=MESH,
    )
    down.start()
    up.start()
    down.wait()
    up.wait()


def kernel_c(own, north, south, vertical, spread, out, wide, fields, edges):
    band = lax.axis_index("wave")
    vertical_stage(band, own, north, south, vertical, spread, out, wide, fields, edges)


VM = pl.BlockSpec(memory_space=pltpu.VMEM)
ANY = pl.BlockSpec(memory_space=pl.ANY)
SM = pl.BlockSpec(memory_space=pltpu.SMEM)


def params(**kw):
    return pltpu.CompilerParams(vmem_limit_bytes=40 * 2**20, **kw)


def body(spectrum, legendre, wave_numbers, vertical):
    spec = jnp.transpose(spectrum, (2, 3, 0, 1)).reshape(COLS, SLOTS, NM)
    shape = jax.ShapeDtypeStruct
    dma = pltpu.SemaphoreType.DMA
    pair = (shape((WAVES, SLOTS, 128), BF), shape((WAVES, 2, 128), F32))
    main, rest = pl.pallas_call(
        kernel_a,
        name="legendre",
        out_shape=pair,
        in_specs=[SM, VM, ANY],
        out_specs=(VM, VM),
        scratch_shapes=[
            pltpu.VMEM((SLOTS, NM, 128), BF),
            dma((4,)),
            pltpu.VMEM((8, 640, 128), F32),
            pltpu.VMEM((2, 2, 128, 128), F32),
            pltpu.VMEM((2, 256, 128), F32),
            pltpu.VMEM((WAVES * SLOTS, 128), F32),
        ],
        compiler_params=params(),
    )(wave_numbers, spec, legendre)
    main, rest = pl.pallas_call(
        kernel_t1,
        name="bands",
        out_shape=pair,
        in_specs=[VM, VM],
        out_specs=(VM, VM),
        scratch_shapes=[dma((2,)), dma((2,)), dma((2,))],
        compiler_params=params(collective_id=0, has_side_effects=True),
    )(main, rest)
    message = pl.pallas_call(
        kernel_b,
        name="fourier",
        out_shape=shape((LEVDEV, 10, 8, 128), BF),
        in_specs=[VM] * 6,
        out_specs=VM,
        scratch_shapes=[
            pltpu.VMEM((NM, NM), BF),
            pltpu.VMEM((NM, 128), F32),
            pltpu.VMEM((NM, 256), BF),
            pltpu.VMEM((RADIX, 72, 2 * SPAN), F32),
            pltpu.VMEM((72, NLON), F32),
            pltpu.VMEM((80, 128), F32),
        ],
        compiler_params=params(),
    )(
        main,
        rest,
        wave_numbers.reshape(1, NM),
        jnp.asarray(row_table()),
        jnp.asarray(fourier_table()),
        jnp.asarray(edge_table()),
    )
    own, north, south = pl.pallas_call(
        kernel_t2,
        name="longitudes",
        out_shape=(
            shape((LEVDEV, 10, 8, 128), BF),
            shape((LEVDEV, 4, 8, 128), BF),
            shape((LEVDEV, 4, 8, 128), BF),
        ),
        in_specs=[VM],
        out_specs=(VM, VM, VM),
        scratch_shapes=[dma(()), dma(()), dma(()), dma((2,)), dma((2,))],
        compiler_params=params(collective_id=1, has_side_effects=True),
    )(message)
    return pl.pallas_call(
        kernel_c,
        name="upwind",
        out_shape=shape((LEVS, 4, 128), F32),
        in_specs=[VM] * 5,
        out_specs=VM,
        scratch_shapes=[
            pltpu.VMEM((5, LEVDEV * 24, 128), F32),
            pltpu.VMEM((5, 4, LEVS, 128), F32),
            pltpu.VMEM((3, LEVS, 128), F32),
        ],
        compiler_params=params(),
    )(own, north, south, vertical, jnp.asarray(spread_table()))


def solution(mesh):
    placed = (P("wave", None, "lev", None), P("wave", None, None), P(), P())
    return jax.shard_map(
        body, mesh=mesh, in_specs=placed, out_specs=P(None, "wave", "lev"), check_vma=False
    )
```

time: 139 us -> 76.4 us (0.55)
  the two profiles are of different devices: /device:TPU:8 before, /device:TPU:1 now
where the time goes in v1:
time: 76.4 us; the launch traced here: 76.1 us
  Pallas kernels  71.8 us (94%)
  local copies, waits for them, and re-layouts  4.17 us (5%)
    pallas_call x1, Pallas kernels, body(): pl.pallas_call(kernel_t1, name='bands', out_shape=pair, in_specs=[VM, VM]...  32.1 us
    pallas_call x1, Pallas kernels, body(): pl.pallas_call(kernel_t2, name='longitudes', out_shape=(shape((LEVDEV, 10...  25.8 us
    pallas_call x1, Pallas kernels, body(): pl.pallas_call(kernel_a, name='legendre', out_shape=pair, in_specs=[SM, V...  4.89 us
    pallas_call x1, Pallas kernels, body(): pl.pallas_call(kernel_b, name='fourier', out_shape=shape((LEVDEV, 10, 8,...  4.74 us
    pallas_call x1, Pallas kernels, body(): pl.pallas_call(kernel_c, name='upwind', out_shape=shape((LEVS, 4, 128), F...  4.28 us
    unnamed x16, local copies, waits for them, and re-layouts  4.17 us

profile of v1, /device:TPU:1, one launch (start us, length us, event | category | flops | bytes accessed | tf_op | source)
XLA Modules:
  0.0 76.1 jit_solution(15494252757523055100)
XLA Ops:
  0.0 0.0 copy-start
  0.0 2.2 %copy-done = bf16[16,1024,128]{2,1,0:T(8,128)(2,1)S(1)} copy-done((bf16[16,1024,128]{2,1,0:T(8,128)(2,1)S(1)}, bf16[16,1024,128]{2,1,0:T(8,128)(2,1)}, u32[]{:S(2)}) %copy-start) | copy-done | bytes 4194328
  2.2 0.0 copy-start.2
  2.2 1.3 %copy-done.2 = bf16[16,1024,6,6]{1,0,3,2:T(8,128)(2,1)S(1)} copy-done((bf16[16,1024,6,6]{1,0,3,2:T(8,128)(2,1)S(1)}, bf16[16,1024,6,6]{1,0,3,2:T(8,128)(2,1)}, u32[]{:S(2)}) %copy-start.2) | copy-done | bytes 1179672
  3.5 0.0 copy-start.7
  3.5 0.7 copy-done.7
  4.1 0.0 copy-start.1
  4.1 0.0 copy-start.3
  4.2 0.0 copy-start.4
  4.2 4.9 %legendre.1 = (bf16[64,16,128]{2,1,0:T(8,128)(2,1)S(1)}, f32[64,2,128]{2,1,0:T(2,128)S(1)}) custom-call(s32[1024]{0:T(1024)S(1)} %copy-done.7, bf16[36,16,1024]{2,1,0:T(8,128)(2,1)S(1)} %bitcast.4, bf16[16,1024,128]{2,1,0:T(8,128)(2,1)S(1)} %copy-done), custom_call_target="tpu_custom_call" | custom-call | tf_op jit(solution)/shard_map/legendre/pallas_call | solution.py:482
  9.1 0.0 copy-start.5
  9.1 0.0 copy-start.6
  9.1 32.1 %bands.1 = (bf16[64,16,128]{2,1,0:T(8,128)(2,1)S(1)}, f32[64,2,128]{2,1,0:T(2,128)S(1)}) custom-call(bf16[64,16,128]{2,1,0:T(8,128)(2,1)S(1)} %get-tuple-element.12.main, f32[64,2,128]{2,1,0:T(2,128)S(1)} %get-tuple-element.13.rest), custom_call_target="tpu_custom_call" | custom-call | tf_op jit(solution)/shard_map/bands/pallas_call | solution.py:498
  41.1 0.0 copy-done.1
  41.2 0.0 copy-done.3
  41.2 0.0 copy-done.4
  41.2 4.7 %fourier.1.message = bf16[16,10,8,128]{3,2,1,0:T(8,128)(2,1)S(1)} custom-call(bf16[64,16,128]{2,1,0:T(8,128)(2,1)S(1)} %get-tuple-element.14.main, f32[64,2,128]{2,1,0:T(2,128)S(1)} %get-tuple-element.15.rest, s32[1,1024]{1,0:T(1,128)S(1)} %bitcast.5, bf16[144,256]{1,0:T(8,128)(2,1)S(1)} %copy-done.4, bf16[8,256,512]{2,1,0:T(8,128)(2,1)S(1)} %copy-done.1, ...), custom_call_target="tpu_custom_call" | custom-call | tf_op jit(solution)/shard_map/fourier/pallas_call | solution.py:507
  45.9 25.8 %longitudes.1 = (bf16[16,10,8,128]{3,2,1,0:T(8,128)(2,1)S(1)}, bf16[16,4,8,128]{3,2,1,0:T(8,128)(2,1)S(1)}, bf16[16,4,8,128]{3,2,1,0:T(8,128)(2,1)S(1)}) custom-call(bf16[16,10,8,128]{3,2,1,0:T(8,128)(2,1)S(1)} %fourier.1.message), custom_call_target="tpu_custom_call" | custom-call | tf_op jit(solution)/shard_map/longitudes/pallas_call | solution.py:530
  71.8 0.0 copy-done.5
  71.8 0.0 copy-done.6
  71.8 4.3 %upwind.1 = f32[96,4,128]{2,1,0:T(4,128)} custom-call(bf16[16,10,8,128]{3,2,1,0:T(8,128)(2,1)S(1)} %get-tuple-element.16.own, bf16[16,4,8,128]{3,2,1,0:T(8,128)(2,1)S(1)} %get-tuple-element.17.north, bf16[16,4,8,128]{3,2,1,0:T(8,128)(2,1)S(1)} %get-tuple-element.18.south, f32[96,96]{1,0:T(8,128)S(1)} %copy-done.5, bf16[96,128]{1,0:T(8,128)(2,1)S(1)} %copy-done.6), custom_call_target="tpu_custom_call" | custom-call | tf_op jit(solution)/shard_map/upwind/pallas_call | solution.py:543
Async XLA Ops:
  0.0 2.2 %copy-start = (bf16[16,1024,128]{2,1,0:T(8,128)(2,1)S(1)}, bf16[16,1024,128]{2,1,0:T(8,128)(2,1)}, u32[]{:S(2)}) copy-start(bf16[16,1024,128]{2,1,0:T(8,128)(2,1)} %leg.1) | copy-start | bytes 12582916
  2.2 1.3 %copy-start.2 = (bf16[16,1024,6,6]{1,0,3,2:T(8,128)(2,1)S(1)}, bf16[16,1024,6,6]{1,0,3,2:T(8,128)(2,1)}, u32[]{:S(2)}) copy-start(bf16[16,1024,6,6]{1,0,3,2:T(8,128)(2,1)} %param.8) | copy-start | bytes 3538948
  3.5 0.7 copy-start.7
  4.1 37.0 %copy-start.1 = (bf16[8,256,512]{2,1,0:T(8,128)(2,1)S(1)}, bf16[8,256,512]{2,1,0:T(8,128)(2,1)}, u32[]{:S(2)}) copy-start(bf16[8,256,512]{2,1,0:T(8,128)(2,1)} %constant.9.clone.table) | copy-start | bytes 6291460
  4.1 37.0 %copy-start.3 = (bf16[2048,128]{1,0:T(8,128)(2,1)S(1)}, bf16[2048,128]{1,0:T(8,128)(2,1)}, u32[]{:S(2)}) copy-start(bf16[2048,128]{1,0:T(8,128)(2,1)} %constant.10.clone.edges) | copy-start | bytes 1572868
  4.2 37.0 %copy-start.4 = (bf16[144,256]{1,0:T(8,128)(2,1)S(1)}, bf16[144,256]{1,0:T(8,128)(2,1)}, u32[]{:S(2)}) copy-start(bf16[144,256]{1,0:T(8,128)(2,1)} %constant.8.clone.order) | copy-start | bytes 221188
  9.1 62.7 %copy-start.5 = (f32[96,96]{1,0:T(8,128)S(1)}, f32[96,96]{1,0:T(8,128)}, u32[]{:S(2)}) copy-start(f32[96,96]{1,0:T(8,128)} %vertical.1) | copy-start | bytes 110596
  9.1 62.7 %copy-start.6 = (bf16[96,128]{1,0:T(8,128)(2,1)S(1)}, bf16[96,128]{1,0:T(8,128)(2,1)}, u32[]{:S(2)}) copy-start(bf16[96,128]{1,0:T(8,128)(2,1)} %constant.11.clone.spread) | copy-start | bytes 73732

commit v2 on v1

--- a/solution.py
+++ b/solution.py
@@ -84,7 +84,7 @@
     return result
 
 
-def legendre_stage(numbers, spec, leg, copies, main, rest, wide, turned, tall, gather):
+def legendre_stage(numbers, spec, leg, arrived, main, rest, wide, turned, tall, gather):
     for c in range(COLS + 4):
         values = spec[c if c < COLS else c - 4].astype(F32)
         for k in range(8):
@@ -94,9 +94,8 @@
     lane = lax.broadcasted_iota(jnp.int32, (32, 128), 1)
     turn = lane // 16 % 4
     small = lane // 4 % 4
-    for s in range(SLOTS):
-        if s % 4 == 0:
-            copies[s // 4].wait()
+
+    def slot(s, j):
         rows = jnp.concatenate(
             [
                 jnp.concatenate(
@@ -117,12 +116,22 @@
         for half in range(2):
             own = sums[half * 40 : (half + 1) * 40]
             block = jnp.concatenate([own[0:16]] * 4 + [own[16:32]] * 4, axis=0)
-            turned[half, s % 2] = block.T
-            lines = [turned[half, s % 2, pl.ds(r, 32, stride=4), :] for r in range(4)]
+            turned[half, j] = block.T
+            lines = [turned[half, j, pl.ds(r, 32, stride=4), :] for r in range(4)]
             if half == 1:
                 lines = lines[::-1]
             gather[pl.ds(half * 512 + s, 32, stride=SLOTS), :] = pick(lines, turn)
-            tall[half, s * 16 : (s + 1) * 16, :] = jnp.concatenate([own[32:40]] * 2, axis=0)
+            tall[half, pl.ds(pl.multiple_of(s * 16, 16), 16), :] = jnp.concatenate(
+                [own[32:40]] * 2, axis=0
+            )
+
+    def group(i, carry):
+        arrived(i)
+        for j in range(4):
+            slot(4 * i + j, j)
+        return carry
+
+    lax.fori_loop(0, 4, group, 0)
     for half in range(2):
         for h in range(2):
             turned[half, h] = tall[half, h * 128 : (h + 1) * 128, :].T
@@ -210,16 +219,11 @@
     lax.fori_loop(0, LEVDEV, pack, 0)
 
 
-def vertical_stage(band, own, north, south, vertical, spread, out, wide, fields, edges):
-    sources = ((own, 0), (own, 3), (own, 7), (north, 1), (south, 0))
-    for i, (ref, tile) in enumerate(sources):
+def modes_to_levels(sources, edge_sources, both, spread_both, wide, fields, edges):
+    for i, ref, tile in sources:
         for d in range(LEVDEV):
             values = ref[d, tile : tile + 3].astype(F32)
             wide[i, d * 24 : (d + 1) * 24, :] = values.reshape(24, 128)
-    top = vertical[...].astype(BF)
-    low = (vertical[...] - top.astype(F32)).astype(BF)
-    both = jnp.concatenate([top, low], axis=0)
-    for i in range(5):
         for q in range(0, 4, 2):
             modes = jnp.concatenate(
                 [wide[i, pl.ds(q, LEVS, stride=4), :], wide[i, pl.ds(q + 1, LEVS, stride=4), :]],
@@ -229,12 +233,12 @@
             value = twice[:LEVS] + twice[LEVS:]
             fields[i, q] = value[:, :128]
             fields[i, q + 1] = value[:, 128:]
-    both = dot(both, spread[...]).astype(BF)
-    for i, (ref, tile) in enumerate(((own, EDGE_TILE), (north, 0), (south, 3))):
-        values = ref[:, tile].reshape(128, 128)
-        twice = dot(both, values)
+    for i, ref, tile in edge_sources:
+        twice = dot(spread_both, ref[:, tile].reshape(128, 128))
         edges[i] = twice[:LEVS] + twice[LEVS:]
 
+
+def upwind_stage(band, fields, edges, out):
     lane = lax.broadcasted_iota(jnp.int32, (8, 128), 1)
     first, last = band == 0, band == WAVES - 1
 
@@ -319,41 +323,75 @@
     lax.fori_loop(0, LEVS // 8, line, 0)
 
 
-def kernel_a(numbers, spec, leg, main, rest, leg_here, sem, wide, turned, tall, gather):
-    copies = []
-    for i in range(4):
-        copy = pltpu.make_async_copy(
-            leg.at[4 * i : 4 * i + 4], leg_here.at[4 * i : 4 * i + 4], sem.at[i]
-        )
-        copy.start()
-        copies.append(copy)
-    first = lax.axis_index("wave") * SLOTS
-    legendre_stage(
-        lambda s: numbers[first + s], spec, leg_here, copies, main, rest, wide, turned, tall, gather
-    )
-
-
 def send_rows(w):
     return jnp.where(w < WAVES // 2, w, 95 - w)
 
 
-def kernel_t1(main, rest, main_out, rest_out, send, recv, here):
-    w = lax.axis_index("wave")
+def all_in_one(
+    numbers_far, line_far, spec_far, leg_far, order_far, table_far, edges_far, vertical_far, spread_far,
+    out,
+    numbers, line, spec, leg, order, table, edges, vertical, spread,
+    load, leg_load,
+    wide, turned, tall, gather, main, rest,
+    main_in, rest_in, choice, small, joined, part, grid, edge, message,
+    own, north, south, modes, fields, rims,
+    send, recv, here, halo_send, halo_recv,
+):
+    w, v = lax.axis_index("wave"), lax.axis_index("lev")
+    loads = [
+        pltpu.make_async_copy(far, near, load.at[i])
+        for i, (far, near) in enumerate(
+            (
+                (numbers_far, numbers),
+                (spec_far, spec),
+                (line_far, line),
+                (order_far, order),
+                (table_far, table),
+                (edges_far, edges),
+                (vertical_far, vertical),
+                (spread_far, spread),
+            )
+        )
+    ]
+
+    def leg_copy(i):
+        rows = pl.ds(4 * i, 4)
+        return pltpu.make_async_copy(leg_far.at[rows], leg.at[rows], leg_load.at[i])
+
+    for copy in loads[:2]:
+        copy.start()
+    for i in range(4):
+        leg_copy(i).start()
+    for copy in loads[2:]:
+        copy.start()
+
     barrier = pltpu.get_barrier_semaphore()
 
-    def greet(i, carry):
-        pl.semaphore_signal(
-            barrier, inc=1, device_id={"wave": lax.rem(w + i, WAVES)}, device_id_type=MESH
-        )
-        return carry
-
-    lax.fori_loop(1, WAVES, greet, 0)
-    pl.semaphore_wait(barrier, WAVES - 1)
-
-    def go(i, carry):
+    def greet(axis, count, own_index):
+        def step(i, carry):
+            other = lax.rem(own_index + i, count)
+            pl.semaphore_signal(barrier, inc=1, device_id={axis: other}, device_id_type=MESH)
+            return carry
+
+        lax.fori_loop(1, count, step, 0)
+
+    greet("wave", WAVES, w)
+    greet("lev", LEVDEV, v)
+    loads[0].wait()
+    loads[1].wait()
+    first = w * SLOTS
+    legendre_stage(
+        lambda s: numbers[first + s],
+        spec, leg, lambda i: leg_copy(i).wait(), main, rest, wide, turned, tall, gather,
+    )
+    pl.semaphore_wait(barrier, WAVES + LEVDEV - 2)
+
+    pairs = ((main, main_in), (rest, rest_in))
+
+    def to_band(i, carry):
         target = lax.rem(w + i, WAVES)
         row = send_rows(target)
-        for j, (src, dst) in enumerate(((main, main_out), (rest, rest_out))):
+        for j, (src, dst) in enumerate(pairs):
             pltpu.make_async_remote_copy(
                 src_ref=src.at[row],
                 dst_ref=dst.at[w],
@@ -364,18 +402,25 @@
             ).start()
         return carry
 
-    lax.fori_loop(1, WAVES, go, 0)
+    lax.fori_loop(1, WAVES, to_band, 0)
     row = send_rows(w)
     local = [
         pltpu.make_async_copy(src.at[row], dst.at[w], here.at[j])
-        for j, (src, dst) in enumerate(((main, main_out), (rest, rest_out)))
+        for j, (src, dst) in enumerate(pairs)
     ]
     for copy in local:
         copy.start()
+    for copy in loads[2:]:
+        copy.wait()
+    choose_rows(line[...], choice)
+    top = vertical[...].astype(BF)
+    low = (vertical[...] - top.astype(F32)).astype(BF)
+    both = jnp.concatenate([top, low], axis=0)
+    spread_both = dot(both, spread[...]).astype(BF)
     for copy in local:
         copy.wait()
     many = pl.ds(0, WAVES - 1)
-    for j, (src, dst) in enumerate(((main, main_out), (rest, rest_out))):
+    for j, (src, dst) in enumerate(pairs):
         whole = pltpu.make_async_remote_copy(
             src_ref=src.at[many],
             dst_ref=dst.at[many],
@@ -387,172 +432,131 @@
         whole.wait_send()
         whole.wait_recv()
 
-
-def kernel_b(main, rest, numbers, order, table, edges, message, choice, small, joined, part, grid, edge):
-    choose_rows(numbers[...], choice)
     fourier_stage(
-        main, rest, choice, order, table, edges, message, small, joined, part, grid, edge
-    )
-
-
-def kernel_t2(message, own, north, south, send, recv, here, halo_send, halo_recv):
-    w, v = lax.axis_index("wave"), lax.axis_index("lev")
-    barrier = pltpu.get_barrier_semaphore()
-
-    def greet(i, carry):
-        pl.semaphore_signal(
-            barrier, inc=1, device_id={"lev": lax.rem(v + i, LEVDEV)}, device_id_type=MESH
-        )
-        return carry
-
-    lax.fori_loop(1, LEVDEV, greet, 0)
-    upper, lower = lax.rem(w + WAVES - 1, WAVES), lax.rem(w + 1, WAVES)
-    for other in (upper, lower):
-        pl.semaphore_signal(barrier, inc=1, device_id={"wave": other}, device_id_type=MESH)
-    pl.semaphore_wait(barrier, LEVDEV + 1)
-
-    def go(i, carry):
+        main_in, rest_in, choice, order, table, edges, message, small, joined, part, grid, edge
+    )
+
+    def to_block(i, carry):
         target = lax.rem(v + i, LEVDEV)
         pltpu.make_async_remote_copy(
             src_ref=message.at[target],
             dst_ref=own.at[v],
-            send_sem=send,
-            recv_sem=recv,
+            send_sem=send.at[2],
+            recv_sem=recv.at[2],
             device_id={"lev": target},
             device_id_type=MESH,
         ).start()
         return carry
 
-    lax.fori_loop(1, LEVDEV, go, 0)
-    local = pltpu.make_async_copy(message.at[v], own.at[v], here)
+    lax.fori_loop(1, LEVDEV, to_block, 0)
+    local = pltpu.make_async_copy(message.at[v], own.at[v], here.at[2])
     local.start()
     local.wait()
     many = pl.ds(0, LEVDEV - 1)
     whole = pltpu.make_async_remote_copy(
         src_ref=message.at[many],
         dst_ref=own.at[many],
-        send_sem=send,
-        recv_sem=recv,
+        send_sem=send.at[2],
+        recv_sem=recv.at[2],
         device_id={"lev": lax.rem(v + 1, LEVDEV)},
         device_id_type=MESH,
     )
     whole.wait_send()
     whole.wait_recv()
-    down = pltpu.make_async_remote_copy(
-        src_ref=own.at[:, 6:10],
-        dst_ref=north,
-        send_sem=halo_send.at[0],
-        recv_sem=halo_recv.at[0],
-        device_id={"wave": lower},
-        device_id_type=MESH,
-    )
-    up = pltpu.make_async_remote_copy(
-        src_ref=own.at[:, 3:7],
-        dst_ref=south,
-        send_sem=halo_send.at[1],
-        recv_sem=halo_recv.at[1],
-        device_id={"wave": upper},
-        device_id_type=MESH,
-    )
-    down.start()
-    up.start()
-    down.wait()
-    up.wait()
-
-
-def kernel_c(own, north, south, vertical, spread, out, wide, fields, edges):
-    band = lax.axis_index("wave")
-    vertical_stage(band, own, north, south, vertical, spread, out, wide, fields, edges)
-
-
-VM = pl.BlockSpec(memory_space=pltpu.VMEM)
-ANY = pl.BlockSpec(memory_space=pl.ANY)
-SM = pl.BlockSpec(memory_space=pltpu.SMEM)
-
-
-def params(**kw):
-    return pltpu.CompilerParams(vmem_limit_bytes=40 * 2**20, **kw)
+    halos = [
+        pltpu.make_async_remote_copy(
+            src_ref=own.at[:, tile : tile + 4],
+            dst_ref=dst,
+            send_sem=halo_send.at[i],
+            recv_sem=halo_recv.at[i],
+            device_id={"wave": lax.rem(w + step, WAVES)},
+            device_id_type=MESH,
+        )
+        for i, (tile, dst, step) in enumerate(((6, north, 1), (3, south, WAVES - 1)))
+    ]
+    for copy in halos:
+        copy.start()
+    modes_to_levels(
+        ((0, own, 0), (1, own, 3), (2, own, 7)),
+        ((0, own, EDGE_TILE),),
+        both, spread_both, modes, fields, rims,
+    )
+    for copy in halos:
+        copy.wait()
+    modes_to_levels(
+        ((3, north, 1), (4, south, 0)),
+        ((1, north, 0), (2, south, 3)),
+        both, spread_both, modes, fields, rims,
+    )
+    upwind_stage(w, fields, rims, out)
 
 
 def body(spectrum, legendre, wave_numbers, vertical):
     spec = jnp.transpose(spectrum, (2, 3, 0, 1)).reshape(COLS, SLOTS, NM)
-    shape = jax.ShapeDtypeStruct
     dma = pltpu.SemaphoreType.DMA
-    pair = (shape((WAVES, SLOTS, 128), BF), shape((WAVES, 2, 128), F32))
-    main, rest = pl.pallas_call(
-        kernel_a,
-        name="legendre",
-        out_shape=pair,
-        in_specs=[SM, VM, ANY],
-        out_specs=(VM, VM),
+    far = pl.BlockSpec(memory_space=pl.ANY)
+    near = pltpu.VMEM
+    message = (LEVDEV, 10, 8, 128)
+    halo = (LEVDEV, 4, 8, 128)
+    return pl.pallas_call(
+        all_in_one,
+        name="synthesis",
+        out_shape=jax.ShapeDtypeStruct((LEVS, 4, 128), F32),
+        in_specs=[far] * 9,
+        out_specs=pl.BlockSpec(memory_space=near),
         scratch_shapes=[
-            pltpu.VMEM((SLOTS, NM, 128), BF),
+            pltpu.SMEM((NM,), jnp.int32),
+            near((1, NM), jnp.int32),
+            near((COLS, SLOTS, NM), BF),
+            near((SLOTS, NM, 128), BF),
+            near((144, 256), BF),
+            near((RADIX, 256, 2 * SPAN), BF),
+            near((NLON, 128), BF),
+            near((LEVS, LEVS), F32),
+            near((LEVS, 128), BF),
+            dma((8,)),
             dma((4,)),
-            pltpu.VMEM((8, 640, 128), F32),
-            pltpu.VMEM((2, 2, 128, 128), F32),
-            pltpu.VMEM((2, 256, 128), F32),
-            pltpu.VMEM((WAVES * SLOTS, 128), F32),
+            near((8, 640, 128), F32),
+            near((2, 4, 128, 128), F32),
+            near((2, 256, 128), F32),
+            near((WAVES * SLOTS, 128), F32),
+            near((WAVES, SLOTS, 128), BF),
+            near((WAVES, 2, 128), F32),
+            near((WAVES, SLOTS, 128), BF),
+            near((WAVES, 2, 128), F32),
+            near((NM, NM), BF),
+            near((NM, 128), F32),
+            near((NM, 256), BF),
+            near((RADIX, 72, 2 * SPAN), F32),
+            near((72, NLON), F32),
+            near((80, 128), F32),
+            near(message, BF),
+            near(message, BF),
+            near(halo, BF),
+            near(halo, BF),
+            near((5, LEVDEV * 24, 128), F32),
+            near((5, 4, LEVS, 128), F32),
+            near((3, LEVS, 128), F32),
+            dma((3,)),
+            dma((3,)),
+            dma((3,)),
+            dma((2,)),
+            dma((2,)),
         ],
-        compiler_params=params(),
-    )(wave_numbers, spec, legendre)
-    main, rest = pl.pallas_call(
-        kernel_t1,
-        name="bands",
-        out_shape=pair,
-        in_specs=[VM, VM],
-        out_specs=(VM, VM),
-        scratch_shapes=[dma((2,)), dma((2,)), dma((2,))],
-        compiler_params=params(collective_id=0, has_side_effects=True),
-    )(main, rest)
-    message = pl.pallas_call(
-        kernel_b,
-        name="fourier",
-        out_shape=shape((LEVDEV, 10, 8, 128), BF),
-        in_specs=[VM] * 6,
-        out_specs=VM,
-        scratch_shapes=[
-            pltpu.VMEM((NM, NM), BF),
-            pltpu.VMEM((NM, 128), F32),
-            pltpu.VMEM((NM, 256), BF),
-            pltpu.VMEM((RADIX, 72, 2 * SPAN), F32),
-            pltpu.VMEM((72, NLON), F32),
-            pltpu.VMEM((80, 128), F32),
-        ],
-        compiler_params=params(),
+        compiler_params=pltpu.CompilerParams(
+            vmem_limit_bytes=60 * 2**20, collective_id=0, has_side_effects=True
+        ),
     )(
-        main,
-        rest,
+        wave_numbers,
         wave_numbers.reshape(1, NM),
+        spec,
+        legendre,
         jnp.asarray(row_table()),
         jnp.asarray(fourier_table()),
         jnp.asarray(edge_table()),
-    )
-    own, north, south = pl.pallas_call(
-        kernel_t2,
-        name="longitudes",
-        out_shape=(
-            shape((LEVDEV, 10, 8, 128), BF),
-            shape((LEVDEV, 4, 8, 128), BF),
-            shape((LEVDEV, 4, 8, 128), BF),
-        ),
-        in_specs=[VM],
-        out_specs=(VM, VM, VM),
-        scratch_shapes=[dma(()), dma(()), dma(()), dma((2,)), dma((2,))],
-        compiler_params=params(collective_id=1, has_side_effects=True),
-    )(message)
-    return pl.pallas_call(
-        kernel_c,
-        name="upwind",
-        out_shape=shape((LEVS, 4, 128), F32),
-        in_specs=[VM] * 5,
-        out_specs=VM,
-        scratch_shapes=[
-            pltpu.VMEM((5, LEVDEV * 24, 128), F32),
-            pltpu.VMEM((5, 4, LEVS, 128), F32),
-            pltpu.VMEM((3, LEVS, 128), F32),
-        ],
-        compiler_params=params(),
-    )(own, north, south, vertical, jnp.asarray(spread_table()))
+        vertical,
+        jnp.asarray(spread_table()),
+    )
 
 
 def solution(mesh):

time: 76.4 us -> 65.7 us (0.86)
  Pallas kernels: 71.8 us -> 63.9 us
  local copies, waits for them, and re-layouts: 4.17 us -> 1.62 us
    pallas_call x5 -> x1, Pallas kernels: 71.8 us -> 63.9 us  [body(): pl.pallas_call(all_in_one, name='synthesis', out_shape=jax.ShapeDtypeStru...]
    unnamed x16 -> x1, local copies, waits for them, and re-layouts: 4.17 us -> 1.62 us
where the time goes in v2:
time: 65.7 us; the launch traced here: 65.5 us
  Pallas kernels  63.9 us (97%)
  local copies, waits for them, and re-layouts  1.62 us (2%)
    pallas_call x1, Pallas kernels, body(): pl.pallas_call(all_in_one, name='synthesis', out_shape=jax.ShapeDtypeStru...  63.9 us
    unnamed x1, local copies, waits for them, and re-layouts  1.62 us

profile of v2, /device:TPU:1, one launch (start us, length us, event | category | flops | bytes accessed | tf_op | source)
XLA Modules:
  0.0 65.5 jit_solution(4062338700227054196)
XLA Ops:
  0.0 63.9 %synthesis.1 = f32[96,4,128]{2,1,0:T(4,128)} custom-call(s32[1024]{0:T(1024)} %numbers_far.1, s32[1,1024]{1,0:T(1,128)} %bitcast.5, bf16[36,16,1024]{2,1,0:T(8,128)(2,1)} %bitcast.4, bf16[16,1024,128]{2,1,0:T(8,128)(2,1)} %leg_far.1, bf16[144,256]{1,0:T(8,128)(2,1)} %constant.8.clone.order_far, bf16[8,256,512]{2,1,0:T(8,128)(2,1)} %constant.9.clone.table_far, ...), custom_call_target="tpu_custom_call" | custom-call | tf_op jit(solution)/shard_map/synthesis/pallas_call | solution.py:501
  63.9 1.6 %copy.10 = f32[96,4,128]{2,1,0:T(4,128)} copy(f32[96,4,128]{2,1,0:T(4,128)} %synthesis.1) | data formatting | bytes 393216

commit v3 on v2

--- a/solution.py
+++ b/solution.py
@@ -138,9 +138,15 @@
             lines = [turned[half, h, pl.ds(r, 32, stride=4), :] for r in range(4)]
             if half == 1:
                 lines = lines[::-1]
-            rest[half * 32 : (half + 1) * 32, h, :] = pick(lines, small)
+            if half == 0:
+                rest[0:32, h, :] = pick(lines, small)
+            else:
+                chosen = pick(lines, small)
+                for b in range(32):
+                    rest[WAVES - 1 - b, h : h + 1, :] = chosen[b : b + 1]
     for b in range(WAVES):
-        main[b] = gather[b * SLOTS : (b + 1) * SLOTS, :].astype(BF)
+        band = b if b < 32 else 95 - b
+        main[band] = gather[b * SLOTS : (b + 1) * SLOTS, :].astype(BF)
 
 
 def choose_rows(numbers, choice):
@@ -155,7 +161,7 @@
     lax.fori_loop(0, 32, step, 0)
 
 
-def fourier_stage(main, rest, choice, order, table, edges, message, small, joined, part, grid, edge):
+def fourier_stage(main, rest, choice, order, table, edges, message, small, joined, part, grid, edge, ready):
     joined[:, 0:128] = main[...].reshape(NM, 128)
     for h in range(2):
         values = rest[:, h, :]
@@ -199,7 +205,11 @@
                 grid[row, u * SPAN + h * 128 : u * SPAN + (h + 1) * 128] = value
         return carry
 
-    lax.fori_loop(0, 9, combine, 0)
+    lax.fori_loop(0, 3, combine, 0)
+    ready(0, 3)
+    lax.fori_loop(3, 6, combine, 0)
+    ready(3, 3)
+    lax.fori_loop(6, 9, combine, 0)
     edge[0:72] = dot(grid[...].astype(BF), edges[...])
     edge[72:80] = jnp.zeros((8, 128), F32)
     lane = lax.broadcasted_iota(jnp.int32, (8, 128), 1) // 8
@@ -217,13 +227,11 @@
         return carry
 
     lax.fori_loop(0, LEVDEV, pack, 0)
-
-
-def modes_to_levels(sources, edge_sources, both, spread_both, wide, fields, edges):
-    for i, ref, tile in sources:
-        for d in range(LEVDEV):
-            values = ref[d, tile : tile + 3].astype(F32)
-            wide[i, d * 24 : (d + 1) * 24, :] = values.reshape(24, 128)
+    ready(6, 4)
+
+
+def modes_to_levels(groups, both, wide, fields):
+    for i in groups:
         for q in range(0, 4, 2):
             modes = jnp.concatenate(
                 [wide[i, pl.ds(q, LEVS, stride=4), :], wide[i, pl.ds(q + 1, LEVS, stride=4), :]],
@@ -233,12 +241,15 @@
             value = twice[:LEVS] + twice[LEVS:]
             fields[i, q] = value[:, :128]
             fields[i, q + 1] = value[:, 128:]
-    for i, ref, tile in edge_sources:
+
+
+def rims_of(sources, spread_both, rims):
+    for i, ref, tile in sources:
         twice = dot(spread_both, ref[:, tile].reshape(128, 128))
-        edges[i] = twice[:LEVS] + twice[LEVS:]
-
-
-def upwind_stage(band, fields, edges, out):
+        rims[i] = twice[:LEVS] + twice[LEVS:]
+
+
+def upwind_stage(band, fields, edges, out, change):
     lane = lax.broadcasted_iota(jnp.int32, (8, 128), 1)
     first, last = band == 0, band == WAVES - 1
 
@@ -315,27 +326,28 @@
         )
         for lat in range(4):
             west, east = beside(once[lat], rim, lat)
-            out[level, lat, :] = upwind(
-                once[lat], west, east, once[lat - 1], once[lat + 1], cx[lat], cy[lat]
+            row = pl.ds(step * 32 + lat, 8, stride=4)
+            out[row, :] = once[lat]
+            change[row, :] = (
+                jnp.maximum(cx[lat], 0.0) * (once[lat] - west)
+                + jnp.minimum(cx[lat], 0.0) * (east - once[lat])
+                + jnp.maximum(cy[lat], 0.0) * (once[lat] - once[lat - 1])
+                + jnp.minimum(cy[lat], 0.0) * (once[lat + 1] - once[lat])
             )
         return carry
 
     lax.fori_loop(0, LEVS // 8, line, 0)
 
 
-def send_rows(w):
-    return jnp.where(w < WAVES // 2, w, 95 - w)
-
-
 def all_in_one(
     numbers_far, line_far, spec_far, leg_far, order_far, table_far, edges_far, vertical_far, spread_far,
-    out,
+    out, change,
     numbers, line, spec, leg, order, table, edges, vertical, spread,
     load, leg_load,
     wide, turned, tall, gather, main, rest,
     main_in, rest_in, choice, small, joined, part, grid, edge, message,
     own, north, south, modes, fields, rims,
-    send, recv, here, halo_send, halo_recv,
+    send, recv, here, block_recv, halo_send, halo_recv,
 ):
     w, v = lax.axis_index("wave"), lax.axis_index("lev")
     loads = [
@@ -389,11 +401,11 @@
     pairs = ((main, main_in), (rest, rest_in))
 
     def to_band(i, carry):
-        target = lax.rem(w + i, WAVES)
-        row = send_rows(target)
+        target = w + i
+        target = jnp.where(target >= WAVES, target - WAVES, target)
         for j, (src, dst) in enumerate(pairs):
             pltpu.make_async_remote_copy(
-                src_ref=src.at[row],
+                src_ref=src.at[target],
                 dst_ref=dst.at[w],
                 send_sem=send.at[j],
                 recv_sem=recv.at[j],
@@ -402,10 +414,9 @@
             ).start()
         return carry
 
-    lax.fori_loop(1, WAVES, to_band, 0)
-    row = send_rows(w)
+    lax.fori_loop(1, WAVES, to_band, 0, unroll=9)
     local = [
-        pltpu.make_async_copy(src.at[row], dst.at[w], here.at[j])
+        pltpu.make_async_copy(src.at[w], dst.at[w], here.at[j])
         for j, (src, dst) in enumerate(pairs)
     ]
     for copy in local:
@@ -432,63 +443,77 @@
         whole.wait_send()
         whole.wait_recv()
 
+    shifts = [8] + [8 + sign * k for k in range(1, 8) for sign in (-1, 1)]
+
+    def other_block(shift):
+        block = v + shift
+        return jnp.where(block >= LEVDEV, block - LEVDEV, block)
+
+    def block_copy(src, dst, shift):
+        return pltpu.make_async_remote_copy(
+            src_ref=message.at[other_block(shift)] if src is None else src,
+            dst_ref=dst,
+            send_sem=send.at[2],
+            recv_sem=block_recv.at[v],
+            device_id={"lev": other_block(shift)},
+            device_id_type=MESH,
+        )
+
+    def ready(tile, count):
+        rows = pl.ds(tile, count)
+        for shift in shifts:
+            block_copy(
+                message.at[other_block(shift), rows], own.at[v, rows], shift
+            ).start()
+
     fourier_stage(
-        main_in, rest_in, choice, order, table, edges, message, small, joined, part, grid, edge
+        main_in, rest_in, choice, order, table, edges, message, small, joined, part, grid, edge, ready
     )
-
-    def to_block(i, carry):
-        target = lax.rem(v + i, LEVDEV)
-        pltpu.make_async_remote_copy(
-            src_ref=message.at[target],
-            dst_ref=own.at[v],
-            send_sem=send.at[2],
-            recv_sem=recv.at[2],
-            device_id={"lev": target},
-            device_id_type=MESH,
-        ).start()
-        return carry
-
-    lax.fori_loop(1, LEVDEV, to_block, 0)
-    local = pltpu.make_async_copy(message.at[v], own.at[v], here.at[2])
-    local.start()
-    local.wait()
-    many = pl.ds(0, LEVDEV - 1)
-    whole = pltpu.make_async_remote_copy(
-        src_ref=message.at[many],
-        dst_ref=own.at[many],
-        send_sem=send.at[2],
-        recv_sem=recv.at[2],
-        device_id={"lev": lax.rem(v + 1, LEVDEV)},
-        device_id_type=MESH,
-    )
-    whole.wait_send()
-    whole.wait_recv()
-    halos = [
-        pltpu.make_async_remote_copy(
-            src_ref=own.at[:, tile : tile + 4],
+    itself = pltpu.make_async_copy(message.at[v], own.at[v], here.at[2])
+    itself.start()
+    itself.wait()
+
+    def halo_copy(i, src, dst):
+        return pltpu.make_async_remote_copy(
+            src_ref=src,
             dst_ref=dst,
             send_sem=halo_send.at[i],
             recv_sem=halo_recv.at[i],
-            device_id={"wave": lax.rem(w + step, WAVES)},
+            device_id={"wave": lax.rem(w + (1 if i == 0 else WAVES - 1), WAVES)},
             device_id_type=MESH,
         )
-        for i, (tile, dst, step) in enumerate(((6, north, 1), (3, south, WAVES - 1)))
-    ]
-    for copy in halos:
-        copy.start()
-    modes_to_levels(
-        ((0, own, 0), (1, own, 3), (2, own, 7)),
-        ((0, own, EDGE_TILE),),
-        both, spread_both, modes, fields, rims,
-    )
-    for copy in halos:
-        copy.wait()
-    modes_to_levels(
-        ((3, north, 1), (4, south, 0)),
-        ((1, north, 0), (2, south, 3)),
-        both, spread_both, modes, fields, rims,
-    )
-    upwind_stage(w, fields, rims, out)
+
+    def pass_on(block):
+        halo_copy(0, own.at[block, pl.ds(6, 4)], north.at[block]).start()
+        halo_copy(1, own.at[block, pl.ds(3, 4)], south.at[block]).start()
+        row = pl.ds(pl.multiple_of(block * 24, 8), 24)
+        for i, tile in enumerate((0, 3, 7)):
+            modes[i, row, :] = own[block, tile : tile + 3].astype(F32).reshape(24, 128)
+
+    pass_on(v)
+    for shift in shifts:
+        block = other_block(LEVDEV - shift)
+        pltpu.make_async_remote_copy(
+            src_ref=message.at[block],
+            dst_ref=own.at[block],
+            send_sem=send.at[2],
+            recv_sem=block_recv.at[block],
+            device_id={"lev": block},
+            device_id_type=MESH,
+        ).wait_recv()
+        pass_on(block)
+    modes_to_levels((0, 1, 2), both, modes, fields)
+    rims_of(((0, own, EDGE_TILE),), spread_both, rims)
+    many = pl.ds(0, LEVDEV - 1)
+    block_copy(message.at[many], own.at[many], 1).wait_send()
+    halo_copy(0, own.at[:, pl.ds(6, 4)], north).wait()
+    halo_copy(1, own.at[:, pl.ds(3, 4)], south).wait()
+    for i, ref, tile in ((3, north, 1), (4, south, 0)):
+        for d in range(LEVDEV):
+            modes[i, d * 24 : (d + 1) * 24, :] = ref[d, tile : tile + 3].astype(F32).reshape(24, 128)
+    modes_to_levels((3, 4), both, modes, fields)
+    rims_of(((1, north, 0), (2, south, 3)), spread_both, rims)
+    upwind_stage(w, fields, rims, out, change)
 
 
 def body(spectrum, legendre, wave_numbers, vertical):
@@ -496,14 +521,15 @@
     dma = pltpu.SemaphoreType.DMA
     far = pl.BlockSpec(memory_space=pl.ANY)
     near = pltpu.VMEM
+    here = pl.BlockSpec(memory_space=pltpu.VMEM)
     message = (LEVDEV, 10, 8, 128)
     halo = (LEVDEV, 4, 8, 128)
-    return pl.pallas_call(
+    before, change = pl.pallas_call(
         all_in_one,
         name="synthesis",
-        out_shape=jax.ShapeDtypeStruct((LEVS, 4, 128), F32),
+        out_shape=(jax.ShapeDtypeStruct((LEVS * 4, 128), F32),) * 2,
         in_specs=[far] * 9,
-        out_specs=pl.BlockSpec(memory_space=near),
+        out_specs=(here, here),
         scratch_shapes=[
             pltpu.SMEM((NM,), jnp.int32),
             near((1, NM), jnp.int32),
@@ -538,8 +564,9 @@
             near((5, 4, LEVS, 128), F32),
             near((3, LEVS, 128), F32),
             dma((3,)),
+            dma((2,)),
             dma((3,)),
-            dma((3,)),
+            dma((LEVDEV,)),
             dma((2,)),
             dma((2,)),
         ],
@@ -557,6 +584,7 @@
         vertical,
         jnp.asarray(spread_table()),
     )
+    return (before - change).reshape(LEVS, 4, 128)
 
 
 def solution(mesh):

time: 65.7 us -> 62.7 us (0.954)
  Pallas kernels: 63.9 us -> 60.8 us
  other arithmetic: 0 us -> 1.72 us
  local copies, waits for them, and re-layouts: 1.62 us -> 0 us
    pallas_call x1, Pallas kernels: 63.9 us -> 60.8 us  [body(): pl.pallas_call(all_in_one, name='synthesis', out_shape=(jax.ShapeDtypeStr...]
    sub x0 -> x1, other arithmetic: none -> 1.72 us  [body(): return (before - change).reshape(LEVS, 4, 128)]
    unnamed x1 -> x0, local copies, waits for them, and re-layouts: 1.62 us -> none
where the time goes in v3:
time: 62.7 us; the launch traced here: 62.5 us
  Pallas kernels  60.8 us (97%)
  other arithmetic  1.72 us (3%)
    pallas_call x1, Pallas kernels, body(): pl.pallas_call(all_in_one, name='synthesis', out_shape=(jax.ShapeDtypeStr...  60.8 us
    sub x1, other arithmetic, body(): return (before - change).reshape(LEVS, 4, 128)  1.72 us

profile of v3, /device:TPU:1, one launch (start us, length us, event | category | flops | bytes accessed | tf_op | source)
XLA Modules:
  0.0 62.5 jit_solution(11171119687562641955)
XLA Ops:
  0.0 60.8 %synthesis.1 = (f32[384,128]{1,0:T(8,128)}, f32[384,128]{1,0:T(8,128)}) custom-call(s32[1024]{0:T(1024)} %numbers_far.1, s32[1,1024]{1,0:T(1,128)} %bitcast.6, bf16[36,16,1024]{2,1,0:T(8,128)(2,1)} %bitcast.5, bf16[16,1024,128]{2,1,0:T(8,128)(2,1)} %leg_far.1, bf16[144,256]{1,0:T(8,128)(2,1)} %constant.8.clone.order_far, ...), custom_call_target="tpu_custom_call" | custom-call | tf_op jit(solution)/shard_map/synthesis/pallas_call | solution.py:527
  60.8 1.7 %sub.3 = f32[384,128]{1,0:T(8,128)} subtract(f32[384,128]{1,0:T(8,128)} %get-tuple-element.7, f32[384,128]{1,0:T(8,128)} %get-tuple-element.8) | non-fusion elementwise | flops 49152 | bytes 589824 | tf_op jit(solution)/shard_map/sub | solution.py:587

commit v4 on v3

--- a/solution.py
+++ b/solution.py
@@ -85,12 +85,13 @@
 
 
 def legendre_stage(numbers, spec, leg, arrived, main, rest, wide, turned, tall, gather):
+    rest[...] = jnp.zeros_like(rest)
     for c in range(COLS + 4):
         values = spec[c if c < COLS else c - 4].astype(F32)
         for k in range(8):
             wide[k, c * SLOTS : (c + 1) * SLOTS, :] = values[:, k * 128 : (k + 1) * 128]
-    degree = lax.broadcasted_iota(jnp.int32, (40, NM), 1)
-    odd = degree % 2 == 1
+    degree = lax.broadcasted_iota(jnp.int32, (1, NM), 1)
+    sign = jnp.where(degree % 2 == 1, -1.0, 1.0)
     lane = lax.broadcasted_iota(jnp.int32, (32, 128), 1)
     turn = lane // 16 % 4
     small = lane // 4 % 4
@@ -110,8 +111,8 @@
             ],
             axis=1,
         )
-        rows = jnp.where(degree < NM - numbers(s), rows, 0.0)
-        both = jnp.concatenate([rows, jnp.where(odd, -rows, rows)], axis=0).astype(BF)
+        counted = jnp.where(degree < NM - numbers(s), 1.0, 0.0)
+        both = jnp.concatenate([rows * counted, rows * (counted * sign)], axis=0).astype(BF)
         sums = dot(both, leg[s])
         for half in range(2):
             own = sums[half * 40 : (half + 1) * 40]
@@ -138,15 +139,11 @@
             lines = [turned[half, h, pl.ds(r, 32, stride=4), :] for r in range(4)]
             if half == 1:
                 lines = lines[::-1]
-            if half == 0:
-                rest[0:32, h, :] = pick(lines, small)
-            else:
-                chosen = pick(lines, small)
-                for b in range(32):
-                    rest[WAVES - 1 - b, h : h + 1, :] = chosen[b : b + 1]
+            rest[pl.ds(half * 256 + h, 32, stride=8), :] = pick(lines, small)
     for b in range(WAVES):
         band = b if b < 32 else 95 - b
-        main[band] = gather[b * SLOTS : (b + 1) * SLOTS, :].astype(BF)
+        main[band, 0:2] = gather[b * SLOTS : (b + 1) * SLOTS, :].astype(BF).reshape(2, 8, 128)
+        main[band, 2] = rest[b * 8 : (b + 1) * 8, :].astype(BF)
 
 
 def choose_rows(numbers, choice):
@@ -162,9 +159,12 @@
 
 
 def fourier_stage(main, rest, choice, order, table, edges, message, small, joined, part, grid, edge, ready):
-    joined[:, 0:128] = main[...].reshape(NM, 128)
+    joined[:, 0:128] = main[:, 0:2].reshape(NM, 128)
+    for i in range(8):
+        tiles = main[i * 8 : (i + 1) * 8, 2].astype(F32)
+        rest[i * 64 : (i + 1) * 64, :] = tiles.reshape(64, 128)
     for h in range(2):
-        values = rest[:, h, :]
+        values = rest[pl.ds(h, WAVES, stride=8), :]
         for g in range(8):
             rolled = values if g == 0 else pltpu.roll(values, 128 - 16 * g, 1)
             small[pl.ds(h * 8 + g, WAVES, stride=SLOTS), :] = rolled
@@ -336,7 +336,7 @@
             )
         return carry
 
-    lax.fori_loop(0, LEVS // 8, line, 0)
+    lax.fori_loop(0, LEVS // 8, line, 0, unroll=2)
 
 
 def all_in_one(
@@ -345,7 +345,7 @@
     numbers, line, spec, leg, order, table, edges, vertical, spread,
     load, leg_load,
     wide, turned, tall, gather, main, rest,
-    main_in, rest_in, choice, small, joined, part, grid, edge, message,
+    main_in, choice, small, joined, part, grid, edge, message,
     own, north, south, modes, fields, rims,
     send, recv, here, block_recv, halo_send, halo_recv,
 ):
@@ -398,29 +398,27 @@
     )
     pl.semaphore_wait(barrier, WAVES + LEVDEV - 2)
 
-    pairs = ((main, main_in), (rest, rest_in))
-
-    def to_band(i, carry):
-        target = w + i
-        target = jnp.where(target >= WAVES, target - WAVES, target)
-        for j, (src, dst) in enumerate(pairs):
-            pltpu.make_async_remote_copy(
-                src_ref=src.at[target],
-                dst_ref=dst.at[w],
-                send_sem=send.at[j],
-                recv_sem=recv.at[j],
-                device_id={"wave": target},
-                device_id_type=MESH,
-            ).start()
-        return carry
-
-    lax.fori_loop(1, WAVES, to_band, 0, unroll=9)
-    local = [
-        pltpu.make_async_copy(src.at[w], dst.at[w], here.at[j])
-        for j, (src, dst) in enumerate(pairs)
-    ]
-    for copy in local:
-        copy.start()
+    x, z = w // 8, lax.rem(w, 8)
+    xs = [jnp.where(x + d >= 8, x + d - 8, x + d) * 8 for d in range(8)]
+    zs = [jnp.where(z + d >= 8, z + d - 8, z + d) for d in range(8)]
+    steps = [(dx, dz) for dx in range(8) for dz in range(8) if dx + dz > 0]
+    steps.sort(key=lambda step: -sum(min(d, 8 - d) for d in step))
+
+    def band_copy(src, dst, target):
+        return pltpu.make_async_remote_copy(
+            src_ref=src,
+            dst_ref=dst,
+            send_sem=send.at[0],
+            recv_sem=recv.at[0],
+            device_id={"wave": target},
+            device_id_type=MESH,
+        )
+
+    for dx, dz in steps:
+        target = xs[dx] + zs[dz]
+        band_copy(main.at[target], main_in.at[w], target).start()
+    local = pltpu.make_async_copy(main.at[w], main_in.at[w], here.at[0])
+    local.start()
     for copy in loads[2:]:
         copy.wait()
     choose_rows(line[...], choice)
@@ -428,20 +426,11 @@
     low = (vertical[...] - top.astype(F32)).astype(BF)
     both = jnp.concatenate([top, low], axis=0)
     spread_both = dot(both, spread[...]).astype(BF)
-    for copy in local:
-        copy.wait()
+    local.wait()
     many = pl.ds(0, WAVES - 1)
-    for j, (src, dst) in enumerate(pairs):
-        whole = pltpu.make_async_remote_copy(
-            src_ref=src.at[many],
-            dst_ref=dst.at[many],
-            send_sem=send.at[j],
-            recv_sem=recv.at[j],
-            device_id={"wave": lax.rem(w + 1, WAVES)},
-            device_id_type=MESH,
-        )
-        whole.wait_send()
-        whole.wait_recv()
+    whole = band_copy(main.at[many], main_in.at[many], xs[1] + zs[0])
+    whole.wait_send()
+    whole.wait_recv()
 
     shifts = [8] + [8 + sign * k for k in range(1, 8) for sign in (-1, 1)]
 
@@ -453,7 +442,7 @@
         return pltpu.make_async_remote_copy(
             src_ref=message.at[other_block(shift)] if src is None else src,
             dst_ref=dst,
-            send_sem=send.at[2],
+            send_sem=send.at[1],
             recv_sem=block_recv.at[v],
             device_id={"lev": other_block(shift)},
             device_id_type=MESH,
@@ -467,9 +456,9 @@
             ).start()
 
     fourier_stage(
-        main_in, rest_in, choice, order, table, edges, message, small, joined, part, grid, edge, ready
+        main_in, rest, choice, order, table, edges, message, small, joined, part, grid, edge, ready
     )
-    itself = pltpu.make_async_copy(message.at[v], own.at[v], here.at[2])
+    itself = pltpu.make_async_copy(message.at[v], own.at[v], here.at[1])
     itself.start()
     itself.wait()
 
@@ -496,7 +485,7 @@
         pltpu.make_async_remote_copy(
             src_ref=message.at[block],
             dst_ref=own.at[block],
-            send_sem=send.at[2],
+            send_sem=send.at[1],
             recv_sem=block_recv.at[block],
             device_id={"lev": block},
             device_id_type=MESH,
@@ -546,10 +535,9 @@
             near((2, 4, 128, 128), F32),
             near((2, 256, 128), F32),
             near((WAVES * SLOTS, 128), F32),
-            near((WAVES, SLOTS, 128), BF),
-            near((WAVES, 2, 128), F32),
-            near((WAVES, SLOTS, 128), BF),
-            near((WAVES, 2, 128), F32),
+            near((WAVES, 3, 8, 128), BF),
+            near((WAVES * 8, 128), F32),
+            near((WAVES, 3, 8, 128), BF),
             near((NM, NM), BF),
             near((NM, 128), F32),
             near((NM, 256), BF),
@@ -563,9 +551,9 @@
             near((5, LEVDEV * 24, 128), F32),
             near((5, 4, LEVS, 128), F32),
             near((3, LEVS, 128), F32),
-            dma((3,)),
             dma((2,)),
-            dma((3,)),
+            dma((1,)),
+            dma((2,)),
             dma((LEVDEV,)),
             dma((2,)),
             dma((2,)),

time: 62.7 us -> 59.4 us (0.947)
  Pallas kernels: 60.8 us -> 57.5 us
    pallas_call x1, Pallas kernels: 60.8 us -> 57.5 us  [body(): pl.pallas_call(all_in_one, name='synthesis', out_shape=(jax.ShapeDtypeStr...]
where the time goes in v4:
time: 59.4 us; the launch traced here: 59.3 us
  Pallas kernels  57.5 us (97%)
  other arithmetic  1.72 us (3%)
    pallas_call x1, Pallas kernels, body(): pl.pallas_call(all_in_one, name='synthesis', out_shape=(jax.ShapeDtypeStr...  57.5 us
    sub x1, other arithmetic, body(): return (before - change).reshape(LEVS, 4, 128)  1.72 us

profile of v4, /device:TPU:1, one launch (start us, length us, event | category | flops | bytes accessed | tf_op | source)
XLA Modules:
  0.0 59.3 jit_solution(18237105264049703138)
XLA Ops:
  0.0 57.5 %synthesis.1 = (f32[384,128]{1,0:T(8,128)}, f32[384,128]{1,0:T(8,128)}) custom-call(s32[1024]{0:T(1024)} %numbers_far.1, s32[1,1024]{1,0:T(1,128)} %bitcast.6, bf16[36,16,1024]{2,1,0:T(8,128)(2,1)} %bitcast.5, bf16[16,1024,128]{2,1,0:T(8,128)(2,1)} %leg_far.1, bf16[144,256]{1,0:T(8,128)(2,1)} %constant.8.clone.order_far, ...), custom_call_target="tpu_custom_call" | custom-call | tf_op jit(solution)/shard_map/synthesis/pallas_call | solution.py:516
  57.5 1.7 %sub.3 = f32[384,128]{1,0:T(8,128)} subtract(f32[384,128]{1,0:T(8,128)} %get-tuple-element.7, f32[384,128]{1,0:T(8,128)} %get-tuple-element.8) | non-fusion elementwise | flops 49152 | bytes 589824 | tf_op jit(solution)/shard_map/sub | solution.py:575

commit v5 on v4

--- a/solution.py
+++ b/solution.py
@@ -59,11 +59,17 @@
 
 
 def edge_table():
-    table = np.zeros((NLON, 128), np.float32)
+    numbers = np.arange(NM).reshape(NM // RADIX, RADIX).T
+    residue = np.zeros((RADIX, NM // RADIX, 128), np.int64)
+    used = np.zeros(128)
     for block in range(LEVDEV):
         for k, offset in enumerate(OFFSETS):
-            table[(block * 128 + offset) % NLON, block * 8 + k] = 1.0
-    return table.astype(BF)
+            residue[:, :, block * 8 + k] = numbers * ((block * 128 + offset) % NLON) % NLON
+            used[block * 8 + k] = 1.0
+    angle = residue * (2.0 * np.pi / NLON)
+    weight = np.where(numbers == 0, 1.0, 2.0)[:, :, None] * used
+    imaginary = np.where(residue % (NLON // 2) == 0, 0.0, weight * np.sin(angle))
+    return np.concatenate([weight * np.cos(angle), -imaginary], axis=1).astype(BF)
 
 
 def spread_table():
@@ -158,7 +164,7 @@
     lax.fori_loop(0, 32, step, 0)
 
 
-def fourier_stage(main, rest, choice, order, table, edges, message, small, joined, part, grid, edge, ready):
+def fourier_stage(main, rest, choice, order, table, edges, message, small, joined, part, edge, ready):
     joined[:, 0:128] = main[:, 0:2].reshape(NM, 128)
     for i in range(8):
         tiles = main[i * 8 : (i + 1) * 8, 2].astype(F32)
@@ -177,6 +183,10 @@
         own = lines[:, k * 128 : (k + 1) * 128]
         pair = jnp.concatenate([own[0:72].astype(BF), own[72:144].astype(BF)], axis=1)
         part[k] = dot(pair, table[k])
+        rim = dot(pair, edges[k])
+        total = rim if k == 0 else total + rim
+    edge[0:72] = total
+    edge[72:80] = jnp.zeros((8, 128), F32)
     root = 0.5**0.5
 
     def combine(i, carry):
@@ -202,16 +212,8 @@
             for u in range(RADIX):
                 value = even[u % 4] + odd[u] if u < 4 else even[u % 4] - odd[u - 4]
                 message[2 * u + h, tile] = value.astype(BF)
-                grid[row, u * SPAN + h * 128 : u * SPAN + (h + 1) * 128] = value
         return carry
 
-    lax.fori_loop(0, 3, combine, 0)
-    ready(0, 3)
-    lax.fori_loop(3, 6, combine, 0)
-    ready(3, 3)
-    lax.fori_loop(6, 9, combine, 0)
-    edge[0:72] = dot(grid[...].astype(BF), edges[...])
-    edge[72:80] = jnp.zeros((8, 128), F32)
     lane = lax.broadcasted_iota(jnp.int32, (8, 128), 1) // 8
 
     def pack(block, carry):
@@ -227,7 +229,12 @@
         return carry
 
     lax.fori_loop(0, LEVDEV, pack, 0)
-    ready(6, 4)
+    lax.fori_loop(3, 6, combine, 0)
+    ready(3, 4, 0)
+    lax.fori_loop(6, 9, combine, 0)
+    ready(7, 3, 0)
+    lax.fori_loop(0, 3, combine, 0)
+    ready(0, 3, 1)
 
 
 def modes_to_levels(groups, both, wide, fields):
@@ -345,7 +352,7 @@
     numbers, line, spec, leg, order, table, edges, vertical, spread,
     load, leg_load,
     wide, turned, tall, gather, main, rest,
-    main_in, choice, small, joined, part, grid, edge, message,
+    main_in, choice, small, joined, part, edge, message,
     own, north, south, modes, fields, rims,
     send, recv, here, block_recv, halo_send, halo_recv,
 ):
@@ -387,7 +394,14 @@
 
         lax.fori_loop(1, count, step, 0)
 
-    greet("wave", WAVES, w)
+    x, z = w // 8, lax.rem(w, 8)
+    xs = [jnp.where(x + d >= 8, x + d - 8, x + d) * 8 for d in range(8)]
+    zs = [jnp.where(z + d >= 8, z + d - 8, z + d) for d in range(8)]
+    steps = [(dx, dz) for dx in range(8) for dz in range(8) if dx + dz > 0]
+    steps.sort(key=lambda step: -sum(min(d, 8 - d) for d in step))
+    for dx, dz in steps:
+        target = xs[dx] + zs[dz]
+        pl.semaphore_signal(barrier, inc=1, device_id={"wave": target}, device_id_type=MESH)
     greet("lev", LEVDEV, v)
     loads[0].wait()
     loads[1].wait()
@@ -397,12 +411,6 @@
         spec, leg, lambda i: leg_copy(i).wait(), main, rest, wide, turned, tall, gather,
     )
     pl.semaphore_wait(barrier, WAVES + LEVDEV - 2)
-
-    x, z = w // 8, lax.rem(w, 8)
-    xs = [jnp.where(x + d >= 8, x + d - 8, x + d) * 8 for d in range(8)]
-    zs = [jnp.where(z + d >= 8, z + d - 8, z + d) for d in range(8)]
-    steps = [(dx, dz) for dx in range(8) for dz in range(8) if dx + dz > 0]
-    steps.sort(key=lambda step: -sum(min(d, 8 - d) for d in step))
 
     def band_copy(src, dst, target):
         return pltpu.make_async_remote_copy(
@@ -438,25 +446,25 @@
         block = v + shift
         return jnp.where(block >= LEVDEV, block - LEVDEV, block)
 
-    def block_copy(src, dst, shift):
+    def block_copy(src, dst, shift, kind):
         return pltpu.make_async_remote_copy(
-            src_ref=message.at[other_block(shift)] if src is None else src,
+            src_ref=src,
             dst_ref=dst,
-            send_sem=send.at[1],
-            recv_sem=block_recv.at[v],
+            send_sem=send.at[1 + kind],
+            recv_sem=block_recv.at[kind, v],
             device_id={"lev": other_block(shift)},
             device_id_type=MESH,
         )
 
-    def ready(tile, count):
+    def ready(tile, count, kind):
         rows = pl.ds(tile, count)
         for shift in shifts:
             block_copy(
-                message.at[other_block(shift), rows], own.at[v, rows], shift
+                message.at[other_block(shift), rows], own.at[v, rows], shift, kind
             ).start()
 
     fourier_stage(
-        main_in, rest, choice, order, table, edges, message, small, joined, part, grid, edge, ready
+        main_in, rest, choice, order, table, edges, message, small, joined, part, edge, ready
     )
     itself = pltpu.make_async_copy(message.at[v], own.at[v], here.at[1])
     itself.start()
@@ -475,26 +483,38 @@
     def pass_on(block):
         halo_copy(0, own.at[block, pl.ds(6, 4)], north.at[block]).start()
         halo_copy(1, own.at[block, pl.ds(3, 4)], south.at[block]).start()
+        widen(block, ((1, 3), (2, 7)))
+
+    def widen(block, pairs):
         row = pl.ds(pl.multiple_of(block * 24, 8), 24)
-        for i, tile in enumerate((0, 3, 7)):
+        for i, tile in pairs:
             modes[i, row, :] = own[block, tile : tile + 3].astype(F32).reshape(24, 128)
+
+    def arrived(block, rows, kind):
+        pltpu.make_async_remote_copy(
+            src_ref=message.at[block, rows],
+            dst_ref=own.at[block, rows],
+            send_sem=send.at[1 + kind],
+            recv_sem=block_recv.at[kind, block],
+            device_id={"lev": block},
+            device_id_type=MESH,
+        ).wait_recv()
 
     pass_on(v)
     for shift in shifts:
         block = other_block(LEVDEV - shift)
-        pltpu.make_async_remote_copy(
-            src_ref=message.at[block],
-            dst_ref=own.at[block],
-            send_sem=send.at[1],
-            recv_sem=block_recv.at[block],
-            device_id={"lev": block},
-            device_id_type=MESH,
-        ).wait_recv()
+        arrived(block, pl.ds(3, 7), 0)
         pass_on(block)
+    widen(v, ((0, 0),))
+    for shift in shifts:
+        block = other_block(LEVDEV - shift)
+        arrived(block, pl.ds(0, 3), 1)
+        widen(block, ((0, 0),))
     modes_to_levels((0, 1, 2), both, modes, fields)
     rims_of(((0, own, EDGE_TILE),), spread_both, rims)
     many = pl.ds(0, LEVDEV - 1)
-    block_copy(message.at[many], own.at[many], 1).wait_send()
+    for kind, rows in enumerate((pl.ds(3, 7), pl.ds(0, 3))):
+        block_copy(message.at[many, rows], own.at[many, rows], 1, kind).wait_send()
     halo_copy(0, own.at[:, pl.ds(6, 4)], north).wait()
     halo_copy(1, own.at[:, pl.ds(3, 4)], south).wait()
     for i, ref, tile in ((3, north, 1), (4, south, 0)):
@@ -526,7 +546,7 @@
             near((SLOTS, NM, 128), BF),
             near((144, 256), BF),
             near((RADIX, 256, 2 * SPAN), BF),
-            near((NLON, 128), BF),
+            near((RADIX, 256, 128), BF),
             near((LEVS, LEVS), F32),
             near((LEVS, 128), BF),
             dma((8,)),
@@ -542,7 +562,6 @@
             near((NM, 128), F32),
             near((NM, 256), BF),
             near((RADIX, 72, 2 * SPAN), F32),
-            near((72, NLON), F32),
             near((80, 128), F32),
             near(message, BF),
             near(message, BF),
@@ -551,10 +570,10 @@
             near((5, LEVDEV * 24, 128), F32),
             near((5, 4, LEVS, 128), F32),
             near((3, LEVS, 128), F32),
-            dma((2,)),
+            dma((3,)),
             dma((1,)),
             dma((2,)),
-            dma((LEVDEV,)),
+            dma((2, LEVDEV)),
             dma((2,)),
             dma((2,)),
         ],

time: 59.4 us -> 60.2 us (1.013)
  Pallas kernels: 57.5 us -> 58.3 us
    pallas_call x1, Pallas kernels: 57.5 us -> 58.3 us  [body(): pl.pallas_call(all_in_one, name='synthesis', out_shape=(jax.ShapeDtypeStr...]
where the time goes in v5:
time: 60.2 us; the launch traced here: 60 us
  Pallas kernels  58.3 us (97%)
  other arithmetic  1.72 us (3%)
    pallas_call x1, Pallas kernels, body(): pl.pallas_call(all_in_one, name='synthesis', out_shape=(jax.ShapeDtypeStr...  58.3 us
    sub x1, other arithmetic, body(): return (before - change).reshape(LEVS, 4, 128)  1.72 us

profile of v5, /device:TPU:1, one launch (start us, length us, event | category | flops | bytes accessed | tf_op | source)
XLA Modules:
  0.0 60.0 jit_solution(8715885153619194034)
XLA Ops:
  0.0 58.3 %synthesis.1 = (f32[384,128]{1,0:T(8,128)}, f32[384,128]{1,0:T(8,128)}) custom-call(s32[1024]{0:T(1024)} %numbers_far.1, s32[1,1024]{1,0:T(1,128)} %bitcast.6, bf16[36,16,1024]{2,1,0:T(8,128)(2,1)} %bitcast.5, bf16[16,1024,128]{2,1,0:T(8,128)(2,1)} %leg_far.1, bf16[144,256]{1,0:T(8,128)(2,1)} %constant.8.clone.order_far, ...), custom_call_target="tpu_custom_call" | custom-call | tf_op jit(solution)/shard_map/synthesis/pallas_call | solution.py:536
  58.3 1.7 %sub.3 = f32[384,128]{1,0:T(8,128)} subtract(f32[384,128]{1,0:T(8,128)} %get-tuple-element.7, f32[384,128]{1,0:T(8,128)} %get-tuple-element.8) | non-fusion elementwise | flops 49152 | bytes 589824 | tf_op jit(solution)/shard_map/sub | solution.py:594

commit v6 on v5

--- a/solution.py
+++ b/solution.py
@@ -228,13 +228,13 @@
         message[block, EDGE_TILE] = total.astype(BF)
         return carry
 
+    lax.fori_loop(0, 3, combine, 0)
+    ready(0, 3)
+    lax.fori_loop(3, 6, combine, 0)
+    ready(3, 3)
     lax.fori_loop(0, LEVDEV, pack, 0)
-    lax.fori_loop(3, 6, combine, 0)
-    ready(3, 4, 0)
     lax.fori_loop(6, 9, combine, 0)
-    ready(7, 3, 0)
-    lax.fori_loop(0, 3, combine, 0)
-    ready(0, 3, 1)
+    ready(6, 4)
 
 
 def modes_to_levels(groups, both, wide, fields):
@@ -446,21 +446,21 @@
         block = v + shift
         return jnp.where(block >= LEVDEV, block - LEVDEV, block)
 
-    def block_copy(src, dst, shift, kind):
+    def block_copy(src, dst, shift):
         return pltpu.make_async_remote_copy(
             src_ref=src,
             dst_ref=dst,
-            send_sem=send.at[1 + kind],
-            recv_sem=block_recv.at[kind, v],
+            send_sem=send.at[1],
+            recv_sem=block_recv.at[v],
             device_id={"lev": other_block(shift)},
             device_id_type=MESH,
         )
 
-    def ready(tile, count, kind):
+    def ready(tile, count):
         rows = pl.ds(tile, count)
         for shift in shifts:
             block_copy(
-                message.at[other_block(shift), rows], own.at[v, rows], shift, kind
+                message.at[other_block(shift), rows], own.at[v, rows], shift
             ).start()
 
     fourier_stage(
@@ -483,38 +483,26 @@
     def pass_on(block):
         halo_copy(0, own.at[block, pl.ds(6, 4)], north.at[block]).start()
         halo_copy(1, own.at[block, pl.ds(3, 4)], south.at[block]).start()
-        widen(block, ((1, 3), (2, 7)))
-
-    def widen(block, pairs):
         row = pl.ds(pl.multiple_of(block * 24, 8), 24)
-        for i, tile in pairs:
+        for i, tile in enumerate((0, 3, 7)):
             modes[i, row, :] = own[block, tile : tile + 3].astype(F32).reshape(24, 128)
 
-    def arrived(block, rows, kind):
+    pass_on(v)
+    for shift in shifts:
+        block = other_block(LEVDEV - shift)
         pltpu.make_async_remote_copy(
-            src_ref=message.at[block, rows],
-            dst_ref=own.at[block, rows],
-            send_sem=send.at[1 + kind],
-            recv_sem=block_recv.at[kind, block],
+            src_ref=message.at[block],
+            dst_ref=own.at[block],
+            send_sem=send.at[1],
+            recv_sem=block_recv.at[block],
             device_id={"lev": block},
             device_id_type=MESH,
         ).wait_recv()
-
-    pass_on(v)
-    for shift in shifts:
-        block = other_block(LEVDEV - shift)
-        arrived(block, pl.ds(3, 7), 0)
         pass_on(block)
-    widen(v, ((0, 0),))
-    for shift in shifts:
-        block = other_block(LEVDEV - shift)
-        arrived(block, pl.ds(0, 3), 1)
-        widen(block, ((0, 0),))
     modes_to_levels((0, 1, 2), both, modes, fields)
     rims_of(((0, own, EDGE_TILE),), spread_both, rims)
     many = pl.ds(0, LEVDEV - 1)
-    for kind, rows in enumerate((pl.ds(3, 7), pl.ds(0, 3))):
-        block_copy(message.at[many, rows], own.at[many, rows], 1, kind).wait_send()
+    block_copy(message.at[many], own.at[many], 1).wait_send()
     halo_copy(0, own.at[:, pl.ds(6, 4)], north).wait()
     halo_copy(1, own.at[:, pl.ds(3, 4)], south).wait()
     for i, ref, tile in ((3, north, 1), (4, south, 0)):
@@ -570,10 +558,10 @@
             near((5, LEVDEV * 24, 128), F32),
             near((5, 4, LEVS, 128), F32),
             near((3, LEVS, 128), F32),
-            dma((3,)),
+            dma((2,)),
             dma((1,)),
             dma((2,)),
-            dma((2, LEVDEV)),
+            dma((LEVDEV,)),
             dma((2,)),
             dma((2,)),
         ],

time: 60.2 us -> 59.3 us (0.985)
  Pallas kernels: 58.3 us -> 57.4 us
    pallas_call x1, Pallas kernels: 58.3 us -> 57.4 us  [body(): pl.pallas_call(all_in_one, name='synthesis', out_shape=(jax.ShapeDtypeStr...]
where the time goes in v6:
time: 59.3 us; the launch traced here: 59.1 us
  Pallas kernels  57.4 us (97%)
  other arithmetic  1.72 us (3%)
    pallas_call x1, Pallas kernels, body(): pl.pallas_call(all_in_one, name='synthesis', out_shape=(jax.ShapeDtypeStr...  57.4 us
    sub x1, other arithmetic, body(): return (before - change).reshape(LEVS, 4, 128)  1.72 us

profile of v6, /device:TPU:1, one launch (start us, length us, event | category | flops | bytes accessed | tf_op | source)
XLA Modules:
  0.0 59.1 jit_solution(11317893793476918387)
XLA Ops:
  0.0 57.4 %synthesis.1 = (f32[384,128]{1,0:T(8,128)}, f32[384,128]{1,0:T(8,128)}) custom-call(s32[1024]{0:T(1024)} %numbers_far.1, s32[1,1024]{1,0:T(1,128)} %bitcast.6, bf16[36,16,1024]{2,1,0:T(8,128)(2,1)} %bitcast.5, bf16[16,1024,128]{2,1,0:T(8,128)(2,1)} %leg_far.1, bf16[144,256]{1,0:T(8,128)(2,1)} %constant.8.clone.order_far, ...), custom_call_target="tpu_custom_call" | custom-call | tf_op jit(solution)/shard_map/synthesis/pallas_call | solution.py:524
  57.4 1.7 %sub.3 = f32[384,128]{1,0:T(8,128)} subtract(f32[384,128]{1,0:T(8,128)} %get-tuple-element.7, f32[384,128]{1,0:T(8,128)} %get-tuple-element.8) | non-fusion elementwise | flops 49152 | bytes 589824 | tf_op jit(solution)/shard_map/sub | solution.py:582
